TPU v7x, 512 devices: a whole 4x8x8 slice. The times are simulated.
512 devices in a mesh: clip: 32 (over y_lo, z, core), src: 16 (over x, y_hi).
Axes of the slice: x: 4, y: 8 (y_hi: 4, y_lo: 2; y = y_hi * 2 + y_lo), z: 8, core: 2. Of those that a mesh axis runs over, the one named last changes fastest.
Arguments:
- mask_field: float32 [64, 512, 512], P('clip'), may hold values from -6 to 6
- dose_code: int32 [64, 8, 512, 512], P('clip', None, 'src'), may hold values from 0 to 15
- target: float32 [64, 512, 512], P('clip', 'src'), may hold values from 0 to 1
- pupil: float32 [2, 64, 64], replicated, may hold values from -4 to 4
- source_index: int32 [32], P('src'), may hold values from 0 to 10200, as said below
- source_weight: float32 [32], P('src'), may hold values from 0.015625 to 0.0625
- tile_count: int32 [16], replicated, may hold values from 1 to 4
Outputs:
- grad_mask: float32 [64, 512, 512], P('clip', 'src')
- grad_source: float32 [32], P('src')
Inputs may be any that keep to these rules, and one draw needn't show every extreme that they name: `source_index`: distinct points of the 101 x 101 grid, numbered row by row.
All inputs are finite; a program needn't handle non-finite values.
Results may differ from a plain program's by a relative error of at most 0.0003.
Values sent between devices are 32-bit elements; how exact they have to be, the bound alone decides.
No kernel may reach another device: no remote copies, remote signals or barrier semaphores. Data moves between devices by JAX's collectives and lax.ppermute only.
A program may use at most 64 MiB of HBM per device.

v0:
```python
import math

import jax
import jax.numpy as jnp
from jax import lax
from jax.sharding import PartitionSpec as P

SOURCE_GRID = 101


highest = lax.Precision.HIGHEST
steepness = 4.0
threshold = 1.0
dose_base = 0.85
dose_step = 0.02


def tables(extent, passband):
    frequency = jnp.arange(2 * passband, dtype=jnp.int32) - passband
    position = jnp.arange(extent, dtype=jnp.int32)
    angles = (frequency[:, None] * position[None, :] % extent).astype(jnp.float32) * (
        2.0 * math.pi / extent
    )
    return (jnp.cos(angles), jnp.sin(angles))


def offsets(source_index, passband):
    middle = SOURCE_GRID // 2
    grid_row = source_index // SOURCE_GRID
    grid_col = source_index % SOURCE_GRID
    row_at = (grid_row - middle) * (passband // 2) // middle + passband // 2
    col_at = (grid_col - middle) * (passband // 2) // middle + passband // 2
    return (row_at, col_at)


def spectrum(images, fwd_pair, width):
    lifted = jnp.einsum("jx,txy->tjy", fwd_pair, images, precision=highest)
    blocks = jnp.einsum("tjy,ky->tjk", lifted, fwd_pair, precision=highest)
    cos_cos = blocks[:, :width, :width]
    cos_sin = blocks[:, :width, width:]
    sin_cos = blocks[:, width:, :width]
    sin_sin = blocks[:, width:, width:]
    return (cos_cos - sin_sin, -(sin_cos + cos_sin))


def to_image(spec_re, spec_im, fwd_cos, fwd_sin, out_cos, out_sin):
    extent = fwd_cos.shape[1]
    right_table = jnp.concatenate(
        [jnp.concatenate([fwd_cos, fwd_sin], 1), jnp.concatenate([-fwd_sin, fwd_cos], 1)], 0
    )
    mixed_pair = jnp.einsum(
        "tjk,ky->tjy", jnp.concatenate([spec_re, spec_im], 2), right_table, precision=highest
    )
    stacked = jnp.concatenate([mixed_pair[..., :extent], mixed_pair[..., extent:]], 1)
    left_table = jnp.concatenate([out_cos, -out_sin], 0)
    return jnp.einsum("jx,tjy->txy", left_table, stacked, precision=highest)


def field_of(halfway, row_cos, row_sin, extent):
    half_re = halfway[..., :extent]
    half_im = halfway[..., extent:]
    stacked = jnp.concatenate(
        [jnp.concatenate([half_re, half_im], 2), jnp.concatenate([-half_im, half_re], 2)], 1
    )
    left_table = jnp.concatenate([row_cos, row_sin], 1)
    return jnp.einsum("xp,tpy->txy", left_table, stacked, precision=highest)


def per_device(mask_field, dose_code, target, pupil, source_index, source_weight, tile_count):
    tile_slots = mask_field.shape[0]
    extent = mask_field.shape[1]
    passband = pupil.shape[1]
    width = 2 * passband
    cosine_table, sine_table = tables(extent, passband)
    fwd_cos = cosine_table / math.sqrt(extent)
    fwd_sin = sine_table / math.sqrt(extent)
    fwd_pair = jnp.concatenate([fwd_cos, fwd_sin], 0)
    back_cos = cosine_table.T / math.sqrt(passband)
    back_sin = sine_table.T / math.sqrt(passband)
    position = lax.axis_index("clip")
    slot_ids = position % 2 * tile_slots + jnp.arange(tile_slots, dtype=jnp.int32)
    live = (slot_ids < tile_count[position // 2]).astype(jnp.float32)
    spec_re, spec_im = spectrum(mask_field, fwd_pair, width)
    pupil_re = pupil[0]
    pupil_im = pupil[1]
    zero_at = jnp.zeros((), jnp.int32)
    dose_value = dose_base + dose_step * dose_code.astype(jnp.float32)
    empty_spec = jnp.zeros((tile_slots, width, width), jnp.float32)

    def windows(row_pos, col_pos):
        row_cos = lax.dynamic_slice(back_cos, (zero_at, row_pos), (extent, passband))
        row_sin = lax.dynamic_slice(back_sin, (zero_at, row_pos), (extent, passband))
        col_cos = lax.dynamic_slice(back_cos, (zero_at, col_pos), (extent, passband))
        col_sin = lax.dynamic_slice(back_sin, (zero_at, col_pos), (extent, passband))
        return (row_cos, row_sin, col_cos, col_sin)

    def point_halfway(row_pos, col_pos, col_cos, col_sin):
        block_re = lax.dynamic_slice(
            spec_re, (zero_at, row_pos, col_pos), (tile_slots, passband, passband)
        )
        block_im = lax.dynamic_slice(
            spec_im, (zero_at, row_pos, col_pos), (tile_slots, passband, passband)
        )
        held_re = pupil_re * block_re - pupil_im * block_im
        held_im = pupil_re * block_im + pupil_im * block_re
        right_table = jnp.concatenate(
            [
                jnp.concatenate([col_cos.T, col_sin.T], 1),
                jnp.concatenate([-col_sin.T, col_cos.T], 1),
            ],
            0,
        )
        return jnp.einsum(
            "tpq,qy->tpy", jnp.concatenate([held_re, held_im], 2), right_table, precision=highest
        )

    def adjoint_step(
        carry, weight, row_pos, col_pos, field_pair, left_table, col_cos, col_sin, slope
    ):
        adj_re, adj_im = carry
        field_re = field_pair[..., :extent]
        field_im = field_pair[..., extent:]
        weight_term = jnp.sum(slope * (field_re * field_re + field_im * field_im))
        pushed = 2.0 * weight * slope
        stacked = jnp.einsum(
            "xp,txy->tpy",
            left_table,
            jnp.concatenate([pushed * field_re, pushed * field_im], 2),
            precision=highest,
        )
        upper = stacked[:, :passband]
        lower = stacked[:, passband:]
        dquad_re = upper[..., :extent] + lower[..., extent:]
        dquad_im = upper[..., extent:] - lower[..., :extent]
        back_table = jnp.concatenate(
            [jnp.concatenate([col_cos, -col_sin], 1), jnp.concatenate([col_sin, col_cos], 1)], 0
        )
        dheld = jnp.einsum(
            "tpy,yq->tpq", jnp.concatenate([dquad_re, dquad_im], 2), back_table, precision=highest
        )
        dheld_re = dheld[..., :passband]
        dheld_im = dheld[..., passband:]
        dspec_re = pupil_re * dheld_re + pupil_im * dheld_im
        dspec_im = pupil_re * dheld_im - pupil_im * dheld_re
        where_at = (zero_at, row_pos, col_pos)
        sizes_at = (tile_slots, passband, passband)
        adj_re = lax.dynamic_update_slice(
            adj_re, lax.dynamic_slice(adj_re, where_at, sizes_at) + dspec_re, where_at
        )
        adj_im = lax.dynamic_update_slice(
            adj_im, lax.dynamic_slice(adj_im, where_at, sizes_at) + dspec_im, where_at
        )
        return ((adj_re, adj_im), weight_term)

    row_at, col_at = offsets(source_index, passband)

    def forward(running, source_item):
        weight, row_pos, col_pos = source_item
        row_cos, row_sin, col_cos, col_sin = windows(row_pos, col_pos)
        halfway = point_halfway(row_pos, col_pos, col_cos, col_sin)
        field_pair = field_of(halfway, row_cos, row_sin, extent)
        source_image = field_pair[..., :extent] ** 2 + field_pair[..., extent:] ** 2
        return (running + weight * source_image, halfway)

    blank = jnp.zeros((tile_slots, extent, extent), jnp.float32)
    partial_value, halfways = lax.scan(forward, blank, (source_weight, row_at, col_at))
    intensity = lax.psum_scatter(partial_value, "src", scatter_dimension=1, tiled=True)
    printed = jax.nn.sigmoid(steepness * (dose_value * intensity[:, None] - threshold))
    slope_rows = live[:, None, None] * jnp.sum(
        2.0 * (printed - target[:, None]) * printed * (1.0 - printed) * steepness * dose_value,
        axis=1,
    )
    slope_full = lax.all_gather(slope_rows, "src", axis=1, tiled=True)

    def backward(carry, source_item):
        weight, row_pos, col_pos, halfway = source_item
        row_cos, row_sin, col_cos, col_sin = windows(row_pos, col_pos)
        field_pair = field_of(halfway, row_cos, row_sin, extent)
        left_table = jnp.concatenate([row_cos, row_sin], 1)
        return adjoint_step(
            carry, weight, row_pos, col_pos, field_pair, left_table, col_cos, col_sin, slope_full
        )

    adjoint, weight_terms = lax.scan(
        backward, (empty_spec, empty_spec), (source_weight, row_at, col_at, halfways)
    )
    adj_re, adj_im = adjoint
    whole_grad = to_image(adj_re, adj_im, fwd_cos, fwd_sin, fwd_cos, fwd_sin)
    grad_mask = lax.psum_scatter(whole_grad, "src", scatter_dimension=1, tiled=True)
    grad_source = lax.psum(weight_terms, "clip") / (extent * extent)
    return (grad_mask, grad_source)


def solution(mesh):
    return jax.shard_map(
        per_device,
        mesh=mesh,
        in_specs=(
            P("clip", None, None),
            P("clip", None, "src", None),
            P("clip", "src", None),
            P(),
            P("src"),
            P("src"),
            P(),
        ),
        out_specs=(P("clip", "src", None), P("src")),
        check_vma=False,
    )
```

profile of v0, /device:TPU:1, one launch (start us, length us, event | category | flops | bytes accessed | tf_op | source)
XLA Modules:
  0.0 563.9 jit_solution(5775450339851956198)
XLA Ops:
  7.2 1.9 sine_multiply_fusion.1
  10.3 1.9 convolution_bitcast_fusion.3
  13.4 43.4 %while.30 = (s32[]{:T(128)}, f32[2,512,512]{1,2,0:T(8,128)}, f32[2,2,64,1024]{3,2,1,0:T(8,128)}, f32[2]{0:T(128)S(1)}, f32[1,64,64]{2,1,0:T(8,128)S(1)}, /*index...) while((s32[]{:T(128)}, f32[2,512,512]{1,2,0:T(8,128)}, ...), condition=%wide.region_1.2_spmd.clone.clone, body=%wide.region_0.1_spmd.clone.clone.sunk | while | flops 1816231936 | bytes 25134072 | solution.py:166
  18.2 1.4 bitcast_dynamic-update-slice_fusion.2
  20.7 1.8 copy.46
  23.7 5.3 convolution_bitcast_fusion.7
  29.6 5.1 fusion.110
  39.6 1.4 bitcast_dynamic-update-slice_fusion.2
  42.1 1.8 copy.46
  45.1 5.3 convolution_bitcast_fusion.7
  51.0 5.8 %fusion.110 = f32[2,512,512]{1,2,0:T(8,128)} fusion(f32[2,512,1024]{1,2,0:T(8,128)} %convolution_bitcast_fusion.7, f32[2,512,512]{1,2,0:T(8,128)} %get-tuple-element.590, f32[]{:T(128)} %bitcast.102, pred[]{:T(512)S(6)} %compare.8), kind=kLoop, calls=%fused_computation.43.clone.1 | loop fusion | flops 3145728 | bytes 8388613 | tf_op jit(solution)/shard_map/while/body/eval_jaxpr/add | solution.py:163
  56.8 4.2 copy.25
  64.9 176.3 %all-reduce.5.cloned.1.call-done = f32[2,512,512]{2,0,1:T(2,128)} async-done(((f32[2,512,512]{2,0,1:T(2,128)}), f32[2,512,512]{2,0,1:T(2,128)}) %all-reduce.5.cloned.1.call-update) | async-done | bytes 2097168
  242.1 1.9 multiply_reduce_fusion.1
  245.3 71.1 %all-gather.2.cloned.1.call-done = f32[2,512,512]{2,0,1:T(2,128)} async-done(((f32[2,32,512]{2,0,1:T(2,128)}), f32[2,512,512]{2,0,1:T(2,128)}) %all-gather.2.cloned.1.call-update) | async-done | bytes 2097168 | tf_op jit(solution)/shard_map/all_gather | solution.py:173
  316.4 4.1 copy.28
  321.9 50.5 %while.29 = (s32[]{:T(128)}, f32[2,128,128]{2,1,0:T(8,128)}, f32[2,128,128]{2,1,0:T(8,128)}, f32[2]{0:T(128)S(1)}, s32[2]{0:T(128)S(1)}, /*index=5*/s32[2]{0:T(1...) while((s32[]{:T(128)}, f32[2,128,128]{2,1,0:T(8,128)}, ...), condition=%wide.region_6.7_spmd.clone, body=%wide.region_4.6_spmd.clone.sunk | while | flops 3429269504 | bytes 49709768 | solution.py:184
  331.4 3.7 convolution_bitcast_fusion.6
  336.3 1.5 multiply_reduce_fusion.3
  337.8 4.6 fusion.106
  343.5 1.4 dynamic_update_slice.25
  344.9 1.4 dynamic_update_slice.24
  356.6 3.7 convolution_bitcast_fusion.6
  361.5 1.5 multiply_reduce_fusion.3
  363.0 4.6 fusion.106
  368.7 1.4 dynamic_update_slice.25
  370.1 1.4 dynamic_update_slice.24
  372.4 2.4 fusion.47
  374.9 3.2 convolution_bitcast_fusion.2
  378.1 4.1 copy.33
  382.3 54.5 %psum.7 = f32[2]{0:T(128)S(1)} all-reduce(f32[2]{0:T(128)S(1)} %get-tuple-element.150), channel_id=1, replica_groups=mesh['clip'=32,'src'=16] {'clip'}, use_global_device_ids=true, to_apply=%region_8.9 | all-reduce | flops 2 | bytes 16 | tf_op jit(solution)/shard_map/psum | solution.py:190
  437.3 118.5 %all-reduce.7.cloned.1.call-done = f32[2,512,512]{2,0,1:T(2,128)} async-done(((f32[2,512,512]{2,0,1:T(2,128)}), f32[2,512,512]{2,0,1:T(2,128)}) %all-reduce.7.cloned.1.call-update) | async-done | bytes 2097168
  (182 shorter events, 35.9 us)
Async XLA Ops:
  7.2 234.0 %all-reduce.5.cloned.1.call-start = ((), (), s32[]{:S(2)}) async-start(), calls=%async_computation.1 | async-start | bytes 4194304
  13.4 4.7 copy-start.10
  13.5 6.2 %copy-start.20 = (f32[2,128,128]{2,1,0:T(8,128)}, f32[2,128,128]{2,1,0:T(8,128)S(1)}, u32[]{:S(2)}) copy-start(f32[2,128,128]{2,1,0:T(8,128)S(1)} %get-tuple-element.613) | copy-start | bytes 393220 | tf_op jit(solution)/shard_map/while
  13.5 6.1 %copy-start.22 = (f32[2,128,128]{2,1,0:T(8,128)}, f32[2,128,128]{2,1,0:T(8,128)S(1)}, u32[]{:S(2)}) copy-start(f32[2,128,128]{2,1,0:T(8,128)S(1)} %get-tuple-element.611) | copy-start | bytes 393220 | tf_op jit(solution)/shard_map/while
  29.6 5.2 copy-start.11
  29.6 5.2 copy-start.13
  29.6 5.2 copy-start.21
  29.6 5.2 copy-start.23
  34.8 4.7 copy-start.10
  34.8 4.7 copy-start.12
  34.8 6.2 %copy-start.20 = (f32[2,128,128]{2,1,0:T(8,128)}, f32[2,128,128]{2,1,0:T(8,128)S(1)}, u32[]{:S(2)}) copy-start(f32[2,128,128]{2,1,0:T(8,128)S(1)} %get-tuple-element.613) | copy-start | bytes 393220 | tf_op jit(solution)/shard_map/while
  34.8 6.2 %copy-start.22 = (f32[2,128,128]{2,1,0:T(8,128)}, f32[2,128,128]{2,1,0:T(8,128)S(1)}, u32[]{:S(2)}) copy-start(f32[2,128,128]{2,1,0:T(8,128)S(1)} %get-tuple-element.611) | copy-start | bytes 393220 | tf_op jit(solution)/shard_map/while
  51.0 5.8 %copy-start.11 = (f32[512,128]{0,1:T(8,128)S(1)}, f32[512,128]{0,1:T(8,128)}, u32[]{:S(2)}) copy-start(f32[512,128]{0,1:T(8,128)} %copy-done.10) | copy-start | bytes 786436 | tf_op jit(solution)/shard_map/while
  51.0 5.8 %copy-start.13 = (f32[512,128]{0,1:T(8,128)S(1)}, f32[512,128]{0,1:T(8,128)}, u32[]{:S(2)}) copy-start(f32[512,128]{0,1:T(8,128)} %copy-done.12) | copy-start | bytes 786436 | tf_op jit(solution)/shard_map/while
  51.0 5.8 %copy-start.21 = (f32[2,128,128]{2,1,0:T(8,128)S(1)}, f32[2,128,128]{2,1,0:T(8,128)}, u32[]{:S(2)}) copy-start(f32[2,128,128]{2,1,0:T(8,128)} %copy-done.20) | copy-start | bytes 393220 | tf_op jit(solution)/shard_map/while
  51.0 5.8 %copy-start.23 = (f32[2,128,128]{2,1,0:T(8,128)S(1)}, f32[2,128,128]{2,1,0:T(8,128)}, u32[]{:S(2)}) copy-start(f32[2,128,128]{2,1,0:T(8,128)} %copy-done.22) | copy-start | bytes 393220 | tf_op jit(solution)/shard_map/while
  61.0 181.0 %copy-start.29 = (f32[2,32,512]{2,1,0:T(8,128)S(1)}, f32[2,32,512]{2,1,0:T(8,128)}, u32[]{:S(2)}) copy-start(f32[2,32,512]{2,1,0:T(8,128)} %param.13) | copy-start | bytes 393220
  61.1 184.0 %copy-start.15 = (f32[512,128]{0,1:T(8,128)S(1)}, f32[512,128]{0,1:T(8,128)}, u32[]{:S(2)}) copy-start(f32[512,128]{0,1:T(8,128)} %copy-done.14) | copy-start | bytes 786436
  61.1 255.3 %all-gather.2.cloned.1.call-start = ((), (), s32[]{:S(2)}) async-start(), calls=%async_computation | async-start | bytes 2228224 | tf_op jit(solution)/shard_map/all_gather | solution.py:173
  244.8 310.9 %all-reduce.7.cloned.1.call-start = ((), (), s32[]{:S(2)}) async-start(), calls=%async_computation.2 | async-start | bytes 4194304
  321.9 6.3 %copy-start.3 = (f32[512,128]{1,0:T(8,128)}, f32[512,128]{1,0:T(8,128)S(1)}, u32[]{:S(2)}) copy-start(f32[512,128]{1,0:T(8,128)S(1)} %get-tuple-element.663) | copy-start | bytes 786436 | tf_op jit(solution)/shard_map/while
  321.9 6.3 %copy-start.5 = (f32[512,128]{1,0:T(8,128)}, f32[512,128]{1,0:T(8,128)S(1)}, u32[]{:S(2)}) copy-start(f32[512,128]{1,0:T(8,128)S(1)} %get-tuple-element.664) | copy-start | bytes 786436 | tf_op jit(solution)/shard_map/while
  331.4 4.8 copy-start.1
  337.7 4.8 copy-start.7
  337.7 4.8 copy-start.8
  337.8 4.8 copy-start.9
  347.1 6.4 %copy-start.3 = (f32[512,128]{1,0:T(8,128)}, f32[512,128]{1,0:T(8,128)S(1)}, u32[]{:S(2)}) copy-start(f32[512,128]{1,0:T(8,128)S(1)} %get-tuple-element.663) | copy-start | bytes 786436 | tf_op jit(solution)/shard_map/while
  347.1 6.3 %copy-start.5 = (f32[512,128]{1,0:T(8,128)}, f32[512,128]{1,0:T(8,128)S(1)}, u32[]{:S(2)}) copy-start(f32[512,128]{1,0:T(8,128)S(1)} %get-tuple-element.664) | copy-start | bytes 786436 | tf_op jit(solution)/shard_map/while
  356.6 4.8 copy-start.1
  363.0 4.8 copy-start.7
  363.0 4.8 copy-start.8
  363.0 4.8 copy-start.9
  (27 other events, 59.7 us)
Sparse Core Ops, SparseCore 0:
  61.2 179.8 all-reduce.4
  244.9 71.4 all-gather.1
  382.4 173.3 all-reduce.6
where the time goes:
time: 573 us; the launch traced here: 564 us
  waiting for transfers between devices  366 us (64%)
  blocking collectives  54.5 us (10%)
  local copies, waits for them, and re-layouts  48.8 us (9%)
  matrix products  40.1 us (7%)
  other arithmetic  23.6 us (4%)
  loops' own time  16 us (3%)
  between operations  14.7 us (3%)
    unnamed x5, waiting for transfers between devices  295 us
    all_gather x1, waiting for transfers between devices, per_device(): slope_full = lax.all_gather(slope_rows, 'src', axis=1, tiled=True)  71.1 us
    psum x1, blocking collectives, per_device(): grad_source = lax.psum(weight_terms, 'clip') / (extent * extent)  54.5 us
    dot_general x4, matrix products, field_of(): return jnp.einsum('xp,tpy->txy', left_table, stacked, precision=highest)  18 us
  transfers between devices with their start and end apart: 3, of which 3 were waited for; matrix products, arithmetic and copies ran while one was open for 1% of the time, Pallas kernels for 0%

commit v1 on v0

v1 whole, which is shorter than its diff:
```python
import functools
import math

import jax
import jax.numpy as jnp
import numpy as np
from jax import lax
from jax.experimental import pallas as pl
from jax.experimental.pallas import tpu as pltpu
from jax.sharding import PartitionSpec as P

SOURCE_GRID = 101
TILE = 512
BAND = 64
WIDTH = 128
SRC = 16
ROWS = TILE // SRC
DOSES = 8
POINTS = 32
CHUNK = 2 * ROWS + 8

f32 = jnp.float32
bf16 = jnp.bfloat16


def halves(table):
    whole = np.asarray(table, np.float32)
    high = whole.astype(jnp.bfloat16)
    low = (whole - high.astype(np.float32)).astype(jnp.bfloat16)
    return high, low


def as_left(table):
    high, low = halves(table)
    return np.concatenate([high, high, low], -1)


def as_right(table):
    high, low = halves(table)
    return np.concatenate([high, low, high], -2)


def angles(frequency, position):
    turns = np.outer(np.asarray(frequency), np.asarray(position)) % TILE
    return turns * (2.0 * math.pi / TILE)


@functools.cache
def constants():
    pixel = np.arange(TILE)
    coarse = np.arange(WIDTH) * (TILE // WIDTH)
    wide = np.arange(WIDTH) - BAND
    narrow = np.arange(BAND)
    held = {}
    fwd = angles(wide, pixel)
    fwd_cos = np.cos(fwd) / math.sqrt(TILE)
    fwd_sin = np.sin(fwd) / math.sqrt(TILE)
    pair = np.concatenate([fwd_cos, fwd_sin], 0)
    held["spec_right"] = np.stack(halves(pair.T))
    held["spec_left"] = np.stack(halves(pair))
    row = angles(pixel, narrow)
    row_cos = np.cos(row) / math.sqrt(BAND)
    row_sin = np.sin(row) / math.sqrt(BAND)
    high, low = halves(np.concatenate([row_cos, row_sin], 1).reshape(SRC, ROWS, WIDTH))
    held["row"] = np.concatenate(
        [np.concatenate([high, high], 2), np.concatenate([low, 0 * low], 2)], 1
    )
    back = np.stack(
        [
            np.concatenate([row_cos[at : at + ROWS].T, row_sin[at : at + ROWS].T], 1)
            for at in range(0, TILE, ROWS)
        ]
    )
    held["row_back"] = as_left(back)
    col = angles(narrow, coarse)
    col_cos = np.cos(col) / math.sqrt(BAND)
    col_sin = np.sin(col) / math.sqrt(BAND)
    table = np.concatenate(
        [np.concatenate([col_cos, col_sin], 1), np.concatenate([-col_sin, col_cos], 1)], 0
    )
    held["col"] = as_right(table)
    held["col_back"] = np.concatenate(halves(table.T), 1)
    gap = pixel[None, :] - coarse[:, None]
    raised = sum(np.cos((2.0 * math.pi / TILE) * (f * gap % TILE)) for f in range(1, BAND))
    raised = (1.0 + 2.0 * raised) / WIDTH
    held["raise"] = as_right(raised)
    held["lower"] = as_right(raised.T)
    order = np.arange(1, BAND + 1)
    even = (np.abs(wide)[:, None] == order).astype(np.float32)
    odd = (wide[:, None] == order).astype(np.float32) - (wide[:, None] == -order)
    none = np.zeros_like(even)
    held["fold"] = np.concatenate(
        [
            np.concatenate([even, none, none, -odd], 1),
            np.concatenate([none, -odd, -even, none], 1),
        ],
        0,
    ).astype(jnp.bfloat16)
    final = angles(order, pixel)
    held["image"] = as_right(np.concatenate([np.cos(final), np.sin(final)], 0) / math.sqrt(TILE))
    return held


def split(value):
    high = value.astype(bf16)
    low = (value - high.astype(f32)).astype(bf16)
    return high, low


def split_cols(value):
    high, low = split(value)
    return jnp.concatenate([high, high, low], 1)


def split_rows(value):
    high, low = split(value)
    return jnp.concatenate([high, low, high], 0)


def mm(left, right):
    return jnp.dot(left, right, preferred_element_type=f32)


def pack_kernel(index_ref, weight_ref, out_ref):
    lane = lax.broadcasted_iota(jnp.int32, out_ref.shape, 2)
    packed = jnp.where(lane == 0, index_ref[0], jnp.where(lane == 1, index_ref[1], 0))
    weights = jnp.where(lane == 2, weight_ref[0], jnp.where(lane == 3, weight_ref[1], 0.0))
    out_ref[...] = packed.astype(f32) + weights


def swap_sign(value, first_half):
    turned = pltpu.roll(value, BAND, 1)
    return jnp.where(first_half, -turned, turned)


def place_of(number):
    point = number.astype(jnp.int32)
    grid_row = (point * 41529) >> 22
    grid_col = point - SOURCE_GRID * grid_row
    return ((grid_row * (16 * 5243)) >> 17, (grid_col * (16 * 5243)) >> 17)


def main_kernel(
    count_ref,
    point_ref,
    pupil_ref,
    mask_hbm,
    right_hbm,
    left_hbm,
    dose_hbm,
    target_hbm,
    raise_hbm,
    lower_hbm,
    col_back_hbm,
    fold_hbm,
    row_hbm,
    row_back_hbm,
    col_hbm,
    out_ref,
    mask_ref,
    right_ref,
    left_ref,
    dose_ref,
    target_ref,
    raise_ref,
    lower_ref,
    col_back_ref,
    fold_ref,
    row_ref,
    row_back_ref,
    col_ref,
    re_ref,
    im_ref,
    half_ref,
    field_ref,
    total_ref,
    slope_ref,
    back_ref,
    adj_ref,
    term_ref,
    sems,
):
    clip = lax.axis_index("clip")
    me = lax.axis_index("src")
    half_tile = TILE // 2
    loads = [
        pltpu.make_async_copy(source, target, sems.at[n])
        for n, (source, target) in enumerate(
            (
                (right_hbm, right_ref),
                (mask_hbm.at[0, :half_tile], mask_ref.at[0, :half_tile]),
                (mask_hbm.at[0, half_tile:], mask_ref.at[0, half_tile:]),
                (left_hbm, left_ref),
                (mask_hbm.at[1, :half_tile], mask_ref.at[1, :half_tile]),
                (mask_hbm.at[1, half_tile:], mask_ref.at[1, half_tile:]),
                (row_hbm.at[me], row_ref),
                (col_hbm, col_ref),
                (dose_hbm, dose_ref),
                (target_hbm, target_ref),
                (raise_hbm, raise_ref),
                (lower_hbm, lower_ref),
                (col_back_hbm, col_back_ref),
                (row_back_hbm.at[me], row_back_ref),
                (fold_hbm, fold_ref),
            )
        )
    ]
    for load in loads:
        load.start()
    first_half = lax.broadcasted_iota(jnp.int32, (BAND, WIDTH), 1) < BAND
    total_ref[...] = jnp.zeros_like(total_ref)
    adj_ref[...] = jnp.zeros_like(adj_ref)
    term_ref[...] = jnp.zeros_like(term_ref)
    rows = 2 * ROWS
    pupil_both = [jnp.concatenate([pupil_ref[n], pupil_ref[n]], 1) for n in range(2)]

    loads[0].wait()
    for t in range(2):
        highs = []
        lows = []
        for part in range(2):
            loads[1 + 3 * t + part].wait()
            high, low = split(mask_ref[t, part * half_tile : (part + 1) * half_tile])
            high, low = split(
                mm(high, right_ref[0]) + mm(high, right_ref[1]) + mm(low, right_ref[0])
            )
            highs.append(high)
            lows.append(low)
        high = jnp.concatenate(highs, 0)
        low = jnp.concatenate(lows, 0)
        if t == 0:
            loads[3].wait()
        blocks = mm(left_ref[0], high) + mm(left_ref[0], low) + mm(left_ref[1], high)
        re_ref[t] = blocks[:WIDTH, :WIDTH] - blocks[WIDTH:, WIDTH:]
        im_ref[t] = -(blocks[WIDTH:, :WIDTH] + blocks[:WIDTH, WIDTH:])
    loads[6].wait()
    loads[7].wait()

    def weight_of(k):
        return point_ref[k >> 1, 0, 2 + (k & 1)]

    def window_of(k):
        return place_of(point_ref[k >> 1, 0, k & 1])

    def windows(step, carry):
        for inner in range(8):
            k = step * 8 + inner
            row_pos, col_pos = window_of(k)
            back = (WIDTH - col_pos) & (WIDTH - 1)
            back_half = (WIDTH + BAND - col_pos) & (WIDTH - 1)
            held = []
            for t in range(2):
                window = jnp.where(
                    first_half,
                    pltpu.roll(re_ref[t, pl.ds(row_pos, BAND), :], back, 1),
                    pltpu.roll(im_ref[t, pl.ds(row_pos, BAND), :], back_half, 1),
                )
                turned = swap_sign(window, first_half)
                pupil_re, pupil_im = pupil_both
                high, low = split(
                    jnp.concatenate(
                        [
                            pupil_re * window + pupil_im * turned,
                            pupil_re * turned - pupil_im * window,
                        ],
                        0,
                    )
                )
                held.append(jnp.concatenate([high, low], 0))
            half = mm(row_ref[...], jnp.concatenate(held, 1))
            half = half[:ROWS] + half[ROWS:]
            half = jnp.concatenate([half[:, :WIDTH], half[:, WIDTH:]], 0)
            half_ref[pl.ds(pl.multiple_of(k * rows, rows), rows), :] = split_cols(half)
        return carry

    lax.fori_loop(0, POINTS // 8, windows, 0)

    def fields(step, carry):
        field = mm(
            half_ref[pl.ds(pl.multiple_of(step * 8 * rows, 8 * rows), 8 * rows), :], col_ref[...]
        )
        total = total_ref[...]
        for inner in range(8):
            k = step * 8 + inner
            one = field[inner * rows : (inner + 1) * rows]
            field_ref[k] = one
            total += weight_of(k) * (
                one[:, :WIDTH] * one[:, :WIDTH] + one[:, WIDTH:] * one[:, WIDTH:]
            )
        total_ref[...] = total
        return carry

    lax.fori_loop(0, POINTS // 8, fields, 0)

    for load in loads[8:]:
        load.wait()
    intensity = mm(split_cols(total_ref[...]), raise_ref[...])
    for t in range(2):
        slot = (clip & 1) * 2 + t
        live = jnp.where(slot < count_ref[clip >> 1], 1.0, 0.0).astype(f32)
        bright = intensity[t * ROWS : (t + 1) * ROWS]
        goal = target_ref[t]
        slope = jnp.zeros((ROWS, TILE), f32)
        for s in range(DOSES):
            dose = 0.85 + 0.02 * dose_ref[t, s].astype(f32)
            printed = 1.0 / (1.0 + jnp.exp(-4.0 * (dose * bright - 1.0)))
            slope += (printed - goal) * (printed * (1.0 - printed)) * dose
        slope_ref[t * ROWS : (t + 1) * ROWS] = (8.0 * live) * slope
    slope_ref[:, :WIDTH] = mm(split_cols(slope_ref[...]), lower_ref[...])

    def columns_back(step, carry):
        slope = slope_ref[:, :WIDTH]
        highs = []
        lows = []
        for inner in range(8):
            k = step * 8 + inner
            field = field_ref[k]
            weighed_re = slope * field[:, :WIDTH]
            weighed_im = slope * field[:, WIDTH:]
            term = jnp.sum(
                weighed_re * field[:, :WIDTH] + weighed_im * field[:, WIDTH:], 0, keepdims=True
            )
            term_ref[step * 4 + inner // 2, 2 + inner % 2 : 3 + inner % 2, :] = term
            twice = 2.0 * weight_of(k)
            high, low = split(jnp.concatenate([twice * weighed_re, twice * weighed_im], 1))
            highs.append(high)
            lows.append(low)
        half = mm(jnp.concatenate(highs, 0), col_back_ref[...])
        rest = mm(jnp.concatenate(lows, 0), col_back_ref[:, :WIDTH])
        back_ref[pl.ds(pl.multiple_of(step * 8 * rows, 8 * rows), 8 * rows), :] = (
            half[:, :WIDTH] + half[:, WIDTH:] + rest
        )
        return carry

    lax.fori_loop(0, POINTS // 8, columns_back, 0)

    def rows_back(step, carry):
        for inner in range(8):
            k = step * 8 + inner
            row_pos, col_pos = window_of(k)
            half = back_ref[pl.ds(pl.multiple_of(k * rows, rows), rows), :]
            turned = -swap_sign(half, first_half)
            pair = jnp.concatenate(
                [
                    split_rows(jnp.concatenate([half[:ROWS], turned[:ROWS]], 0)),
                    split_rows(jnp.concatenate([half[ROWS:], turned[ROWS:]], 0)),
                ],
                1,
            )
            both = mm(row_back_ref[...], pair)
            for t in range(2):
                held = both[:, t * WIDTH : (t + 1) * WIDTH]
                spread = pupil_both[0] * held - pupil_both[1] * swap_sign(held, first_half)
                spread_re = pltpu.roll(jnp.where(first_half, spread, 0.0), col_pos, 1)
                spread_im = pltpu.roll(jnp.where(first_half, 0.0, spread), col_pos + BAND, 1)
                adj_ref[t, pl.ds(row_pos, BAND), :] += spread_re
                adj_ref[2 + t, pl.ds(row_pos, BAND), :] += spread_im
        return carry

    lax.fori_loop(0, POINTS // 8, rows_back, 0)

    lane = lax.broadcasted_iota(jnp.int32, (WIDTH, WIDTH), 1)
    tops = []
    bottoms = []
    top_flat = jnp.zeros((WIDTH, WIDTH), f32)
    bottom_flat = jnp.zeros((WIDTH, WIDTH), f32)
    for t in range(2):
        adj_re = adj_ref[t]
        adj_im = adj_ref[2 + t]
        high, low = split(jnp.concatenate([adj_re, adj_im], 1))
        folded = mm(high, fold_ref[...]) + mm(low, fold_ref[...])
        tops.append(folded[:, :WIDTH])
        bottoms.append(folded[:, WIDTH:])
        top_flat += jnp.where(lane == t, pltpu.roll(adj_re, BAND + t, 1), 0.0)
        bottom_flat -= jnp.where(lane == t, pltpu.roll(adj_im, BAND + t, 1), 0.0)
    high, low = split(
        jnp.concatenate(
            [
                jnp.concatenate(tops + [top_flat], 1),
                jnp.concatenate(bottoms + [bottom_flat], 1),
            ],
            0,
        )
    )
    for block in range(4):
        at_rows = slice(block * WIDTH, (block + 1) * WIDTH)
        table_high = right_ref[0, at_rows, :]
        lines = mm(table_high, high) + mm(table_high, low) + mm(right_ref[1, at_rows, :], high)
        flat = lines[:, 2 * WIDTH :].T
        for n in range(4):
            owner = block * 4 + n
            own_rows = lines[n * ROWS : (n + 1) * ROWS]
            out_ref[owner, :ROWS, :] = own_rows[:, :WIDTH]
            out_ref[owner, ROWS:rows, :] = own_rows[:, WIDTH : 2 * WIDTH]
            out_ref[owner, rows:, :] = flat[:8] + term_ref[owner]


def image_kernel(chunk_ref, table_ref, out_ref, term_ref):
    me = lax.axis_index("src")
    rows = 2 * ROWS
    total = jnp.sum(chunk_ref[...], 0)
    image = mm(split_cols(total[:rows]), table_ref[...])
    last = total[rows:]
    flat = pltpu.roll(last, (WIDTH - (me & 3) * ROWS) & (WIDTH - 1), 1)
    diagonal = lax.broadcasted_iota(jnp.int32, (ROWS, WIDTH), 0) == lax.broadcasted_iota(
        jnp.int32, (ROWS, WIDTH), 1
    )
    for t in range(2):
        column = jnp.sum(jnp.where(diagonal, flat[t : t + 1], 0.0), 1, keepdims=True)
        out_ref[t] = image[t * ROWS : (t + 1) * ROWS] + column * (1.0 / math.sqrt(TILE))
    sums = jnp.sum(last, 1, keepdims=True) * (1.0 / (TILE * TILE))
    term_ref[...] = jnp.broadcast_to(jnp.broadcast_to(sums, (8, WIDTH))[None], term_ref.shape)


def whole(array):
    return pl.BlockSpec(array.shape, lambda *_: (0,) * array.ndim)


def clip_groups(clips, bits):
    rest = [c for c in range(clips) if not c & bits]
    return [[base | c for c in range(clips) if not c & ~bits] for base in rest]


def per_device(
    clips, mask_field, dose_code, target, pupil, source_index, source_weight, tile_count
):
    held = {name: jnp.asarray(table) for name, table in constants().items()}
    smem = pl.BlockSpec(memory_space=pltpu.SMEM)
    hbm = pl.BlockSpec(memory_space=pltpu.HBM)

    mine = pl.pallas_call(
        pack_kernel,
        in_specs=[smem, smem],
        out_shape=jax.ShapeDtypeStruct((SRC, 8, WIDTH), f32),
        name="pack",
    )(source_index, source_weight)
    points = lax.all_to_all(mine, "src", 0, 0)

    tables = [
        held[n]
        for n in (
            "spec_right",
            "spec_left",
            "raise",
            "lower",
            "col_back",
            "fold",
            "row",
            "row_back",
            "col",
        )
    ]
    stored = [mask_field, *tables[:2], dose_code, target, *tables[2:]]
    landing = [
        pltpu.VMEM(a.shape[1:] if n in (9, 10) else a.shape, a.dtype)
        for n, a in enumerate(stored)
    ]
    blocks = pl.pallas_call(
        main_kernel,
        in_specs=[smem, smem, whole(pupil)] + [hbm] * len(stored),
        out_shape=jax.ShapeDtypeStruct((SRC, CHUNK, WIDTH), f32),
        scratch_shapes=landing
        + [
            pltpu.VMEM((2, WIDTH, WIDTH), f32),
            pltpu.VMEM((2, WIDTH, WIDTH), f32),
            pltpu.VMEM((POINTS * 2 * ROWS, 3 * WIDTH), bf16),
            pltpu.VMEM((POINTS, 2 * ROWS, 2 * WIDTH), f32),
            pltpu.VMEM((2 * ROWS, WIDTH), f32),
            pltpu.VMEM((2 * ROWS, TILE), f32),
            pltpu.VMEM((POINTS * 2 * ROWS, WIDTH), f32),
            pltpu.VMEM((4, WIDTH, WIDTH), f32),
            pltpu.VMEM((SRC, 8, WIDTH), f32),
            pltpu.SemaphoreType.DMA((len(stored) + 3,)),
        ],
        compiler_params=pltpu.CompilerParams(vmem_limit_bytes=30 * 1024 * 1024),
        cost_estimate=pl.CostEstimate(
            flops=3_000_000_000, bytes_accessed=5_000_000, transcendentals=300_000
        ),
        name="fields",
    )(tile_count, points, pupil, *stored)

    chunks = lax.all_to_all(blocks, "src", 0, 0)
    near = 4 if clips == 32 else 1
    grad_mask, term = pl.pallas_call(
        image_kernel,
        out_shape=[
            jax.ShapeDtypeStruct((2, ROWS, TILE), f32),
            jax.ShapeDtypeStruct((near, 8, WIDTH), f32),
        ],
        compiler_params=pltpu.CompilerParams(vmem_limit_bytes=12 * 1024 * 1024),
        cost_estimate=pl.CostEstimate(
            flops=100_000_000, bytes_accessed=1_000_000, transcendentals=0
        ),
        name="image",
    )(chunks, held["image"])
    if clips == 32:
        term = lax.all_to_all(term, "clip", 0, 0, axis_index_groups=clip_groups(clips, 17))
        term = jnp.broadcast_to(jnp.sum(term, 0), (8, 8, WIDTH))
        term = lax.all_to_all(term, "clip", 0, 0, axis_index_groups=clip_groups(clips, 14))
    grad_source = jnp.sum(term[:, 2:4, 0], 0)
    return (grad_mask, grad_source)


def solution(mesh):
    return jax.shard_map(
        functools.partial(per_device, mesh.shape["clip"]),
        mesh=mesh,
        in_specs=(
            P("clip", None, None),
            P("clip", None, "src", None),
            P("clip", "src", None),
            P(),
            P("src"),
            P("src"),
            P(),
        ),
        out_specs=(P("clip", "src", None), P("src")),
        check_vma=False,
    )
```

time: 573 us -> 101 us (0.18); the launches traced: 564 us -> 100 us
  waiting for transfers between devices: 366 us -> 0 us
  matrix products: 40.1 us -> 0 us
  local copies, waits for them, and re-layouts: 48.8 us -> 14.1 us
  other arithmetic: 23.6 us -> 0.64 us
  Pallas kernels: 0 us -> 19.6 us
  loops' own time: 16 us -> 0 us
  between operations: 14.7 us -> 0.66 us
  blocking collectives: 54.5 us -> 65.2 us
    unnamed x5 -> x0, waiting for transfers between devices: 295 us -> none
    all_gather x1 -> x0, waiting for transfers between devices: 71.1 us -> none  [per_device(): slope_full = lax.all_gather(slope_rows, 'src', axis=1, tiled=True)]
    all_to_all x0 -> x4, blocking collectives: none -> 65.2 us  [the longest x1 21.2 us: per_device(): chunks = lax.all_to_all(blocks, 'src', 0, 0)]
    psum x1 -> x0, blocking collectives: 54.5 us -> none  [per_device(): grad_source = lax.psum(weight_terms, 'clip') / (extent * extent)]
    dot_general x14 -> x0, matrix products: 40.1 us -> none  [the longest x4 18 us: field_of(): return jnp.einsum('xp,tpy->txy', left_table, stacked, precision=highest)]
    pallas_call x0 -> x3, Pallas kernels: none -> 19.6 us  [the longest x1 17.4 us: per_device(): pl.pallas_call(main_kernel, in_specs=[smem, smem, whole(pupil)] + [hbm] *...]
    another operation x2 -> x0, loops' own time: 16 us -> none  [the longest x1 9.16 us: per_device(): lax.scan(backward, (empty_spec, empty_spec), (source_weight, row_at, col_...]
    dynamic_slice x19 -> x0, local copies, waits for them, and re-layouts: 14.7 us -> none  [the longest x12 7.41 us: per_device(): lax.scan(forward, blank, (source_weight, row_at, col_at))]
  transfers between devices with their start and end apart: 3 -> 0, of which waited for: 3 -> 0; matrix products, arithmetic and copies ran while one was open for 1% -> 0% of each run, Pallas kernels for 0% -> 0%
where the time goes in v1:
time: 101 us; the launch traced here: 100 us
  blocking collectives  65.2 us (65%)
  Pallas kernels  19.6 us (19%)
  local copies, waits for them, and re-layouts  14.1 us (14%)
    all_to_all x1, blocking collectives, per_device(): chunks = lax.all_to_all(blocks, 'src', 0, 0)  21.2 us
    all_to_all x1, blocking collectives, per_device(): points = lax.all_to_all(mine, 'src', 0, 0)  19.2 us
    pallas_call x1, Pallas kernels, per_device(): pl.pallas_call(main_kernel, in_specs=[smem, smem, whole(pupil)] + [hbm] *...  17.4 us
    all_to_all x1, blocking collectives, per_device(): lax.all_to_all(term, 'clip', 0, 0, axis_index_groups=clip_groups(clips, 14))  16.7 us
    unnamed x30, local copies, waits for them, and re-layouts  14.1 us
    all_to_all x1, blocking collectives, per_device(): lax.all_to_all(term, 'clip', 0, 0, axis_index_groups=clip_groups(clips, 17))  8.08 us

profile of v1, /device:TPU:1, one launch (start us, length us, event | category | flops | bytes accessed | tf_op | source)
XLA Modules:
  0.0 100.2 jit_solution(14824542217536942243)
XLA Ops:
  0.6 1.3 %pack.1 = f32[16,8,128]{2,1,0:T(8,128)} custom-call(s32[2]{0:T(128)} %index_ref.1, f32[2]{0:T(128)} %weight_ref.1), custom_call_target="tpu_custom_call" | custom-call | tf_op jit(solution)/shard_map/pack/pallas_call | solution.py:431
  1.9 19.2 %all_to_all.20.point_ref = f32[16,8,128]{2,1,0:T(8,128)S(1)} all-to-all(f32[16,8,128]{2,1,0:T(8,128)} %pack.1), channel_id=1, replica_groups=mesh['clip'=32,'src'=16] {'src'}, dimensions={0} | all-to-all | bytes 131072 | tf_op jit(solution)/shard_map/all_to_all | solution.py:437
  21.2 1.6 %copy-done.1 = f32[2,512,512]{2,1,0:T(8,128)S(1)} copy-done((f32[2,512,512]{2,1,0:T(8,128)S(1)}, f32[2,512,512]{2,1,0:T(8,128)}, u32[]{:S(2)}) %copy-start.1) | copy-done | bytes 2097176
  22.8 0.0 copy-start.2
  22.8 1.2 %copy-done.2 = s32[2,8,32,512]{3,2,1,0:T(8,128)S(1)} copy-done((s32[2,8,32,512]{3,2,1,0:T(8,128)S(1)}, s32[2,8,32,512]{3,2,1,0:T(8,128)}, u32[]{:S(2)}) %copy-start.2) | copy-done | bytes 1048600
  24.0 0.0 copy-start.3
  24.0 0.9 copy-done.3
  24.9 0.0 copy-start.4
  24.9 0.8 copy-done.4
  25.7 0.0 copy-start.5
  25.7 0.7 copy-done.5
  26.4 0.0 copy-start.6
  26.4 1.0 %copy-done.6 = bf16[16,64,192]{2,1,0:T(8,128)(2,1)S(1)} copy-done((bf16[16,64,192]{2,1,0:T(8,128)(2,1)S(1)}, bf16[16,64,192]{2,1,0:T(8,128)(2,1)}, u32[]{:S(2)}) %copy-start.6) | copy-done | bytes 393240
  27.4 1.0 %copy-done.7 = bf16[16,64,256]{2,1,0:T(8,128)(2,1)S(1)} copy-done((bf16[16,64,256]{2,1,0:T(8,128)(2,1)S(1)}, bf16[16,64,256]{2,1,0:T(8,128)(2,1)}, u32[]{:S(2)}) %copy-start.7) | copy-done | bytes 524312
  28.5 0.0 copy-start.8
  28.5 1.0 %copy-done.8 = bf16[2,256,512]{2,1,0:T(8,128)(2,1)S(1)} copy-done((bf16[2,256,512]{2,1,0:T(8,128)(2,1)S(1)}, bf16[2,256,512]{2,1,0:T(8,128)(2,1)}, u32[]{:S(2)}) %copy-start.8) | copy-done | bytes 524312
  29.5 0.0 copy-start.9
  29.5 1.0 %copy-done.9 = bf16[2,512,256]{2,1,0:T(8,128)(2,1)S(1)} copy-done((bf16[2,512,256]{2,1,0:T(8,128)(2,1)S(1)}, bf16[2,512,256]{2,1,0:T(8,128)(2,1)}, u32[]{:S(2)}) %copy-start.9) | copy-done | bytes 524312
  30.6 0.0 copy-start.10
  30.6 1.0 copy-done.10
  31.6 0.0 copy-start.11
  31.6 1.0 copy-done.11
  32.6 0.9 copy-done.12
  33.5 0.9 copy-done.13
  34.4 0.9 copy-done.14
  35.3 17.4 %fields.1 = f32[16,72,128]{2,1,0:T(8,128)S(1)} custom-call(s32[16]{0:T(128)S(1)} %copy-done.5, f32[16,8,128]{2,1,0:T(8,128)S(1)} %all_to_all.20.point_ref, f32[2,64,64]{2,1,0:T(8,128)S(1)} %copy-done.4, f32[2,512,512]{2,1,0:T(8,128)S(1)} %copy-done.1, bf16[2,512,256]{2,1,0:T(8,128)(2,1)S(1)} %copy-done.9, bf16[2,256,512]{2,1,0:T(8,128)(2,1)S(1)} %copy-done.8, ...), custom_call_target="tpu_custom_call" | custom-call | flops 3000000000 | bytes 5000000 | tf_op jit(solution)/shard_map/fields/pallas_call | solution.py:458
  52.7 21.2 %all_to_all.21.chunk_ref = f32[16,72,128]{2,1,0:T(8,128)S(1)} all-to-all(f32[16,72,128]{2,1,0:T(8,128)S(1)} %fields.1), channel_id=1, replica_groups=mesh['clip'=32,'src'=16] {'src'}, dimensions={0} | all-to-all | bytes 1179648 | tf_op jit(solution)/shard_map/all_to_all | solution.py:482
  73.9 0.0 copy-done
  73.9 0.9 image.1
  74.8 8.1 %all_to_all.22 = f32[4,8,128]{2,1,0:T(8,128)S(1)} all-to-all(f32[4,8,128]{2,1,0:T(8,128)S(1)} %get-tuple-element.5), channel_id=1, replica_groups={{0,16,256,272},{32,48,288,304},{64,80,320,336},{96,112,352,368},{128,14..., dimensions={0} | all-to-all | bytes 32768 | tf_op jit(solution)/shard_map/all_to_all | solution.py:497
  82.8 16.7 %all_to_all.23 = f32[8,8,128]{2,1,0:T(8,128)S(1)} all-to-all(f32[8,8,128]{2,1,0:T(8,128)S(1)} %broadcast_in_dim.3), channel_id=1, replica_groups={{0,32,64,96,128,160,192,224},{16,48,80,112,144,176,208,240},{256,288,32..., dimensions={0} | all-to-all | bytes 65536 | tf_op jit(solution)/shard_map/all_to_all | solution.py:499
  99.6 0.6 slice_reduce_fusion
  (8 shorter events, 0.0 us)
Async XLA Ops:
  21.2 1.6 %copy-start.1 = (f32[2,512,512]{2,1,0:T(8,128)S(1)}, f32[2,512,512]{2,1,0:T(8,128)}, u32[]{:S(2)}) copy-start(f32[2,512,512]{2,1,0:T(8,128)} %mask_hbm.1) | copy-start | bytes 6291460
  22.8 1.2 %copy-start.2 = (s32[2,8,32,512]{3,2,1,0:T(8,128)S(1)}, s32[2,8,32,512]{3,2,1,0:T(8,128)}, u32[]{:S(2)}) copy-start(s32[2,8,32,512]{3,2,1,0:T(8,128)} %dose_hbm.1) | copy-start | bytes 3145732
  24.0 0.9 copy-start.3
  24.9 0.8 copy-start.4
  25.7 0.7 copy-start.5
  26.4 1.0 %copy-start.6 = (bf16[16,64,192]{2,1,0:T(8,128)(2,1)S(1)}, bf16[16,64,192]{2,1,0:T(8,128)(2,1)}, u32[]{:S(2)}) copy-start(bf16[16,64,192]{2,1,0:T(8,128)(2,1)} %constant.25.clone.row_back_hbm) | copy-start | bytes 1179652
  27.4 1.0 %copy-start.7 = (bf16[16,64,256]{2,1,0:T(8,128)(2,1)S(1)}, bf16[16,64,256]{2,1,0:T(8,128)(2,1)}, u32[]{:S(2)}) copy-start(bf16[16,64,256]{2,1,0:T(8,128)(2,1)} %constant.24.clone.row_hbm) | copy-start | bytes 1572868
  28.5 1.0 %copy-start.8 = (bf16[2,256,512]{2,1,0:T(8,128)(2,1)S(1)}, bf16[2,256,512]{2,1,0:T(8,128)(2,1)}, u32[]{:S(2)}) copy-start(bf16[2,256,512]{2,1,0:T(8,128)(2,1)} %constant.23.clone.left_hbm) | copy-start | bytes 1572868
  29.5 1.0 %copy-start.9 = (bf16[2,512,256]{2,1,0:T(8,128)(2,1)S(1)}, bf16[2,512,256]{2,1,0:T(8,128)(2,1)}, u32[]{:S(2)}) copy-start(bf16[2,512,256]{2,1,0:T(8,128)(2,1)} %constant.22.clone.right_hbm) | copy-start | bytes 1572868
  30.6 1.0 copy-start.10
  31.6 1.0 copy-start.11
  32.6 0.9 copy-start.12
  33.5 0.9 copy-start.13
  34.4 0.9 copy-start.14
  35.3 38.6 %copy-start = (bf16[384,512]{1,0:T(8,128)(2,1)S(1)}, bf16[384,512]{1,0:T(8,128)(2,1)}, u32[]{:S(2)}) copy-start(bf16[384,512]{1,0:T(8,128)(2,1)} %constant.31.clone.table_ref) | copy-start | bytes 1179652

commit v2 on v1

--- a/solution.py
+++ b/solution.py
@@ -61,17 +61,22 @@
     row = angles(pixel, narrow)
     row_cos = np.cos(row) / math.sqrt(BAND)
     row_sin = np.sin(row) / math.sqrt(BAND)
-    high, low = halves(np.concatenate([row_cos, row_sin], 1).reshape(SRC, ROWS, WIDTH))
-    held["row"] = np.concatenate(
-        [np.concatenate([high, high], 2), np.concatenate([low, 0 * low], 2)], 1
-    )
-    back = np.stack(
-        [
-            np.concatenate([row_cos[at : at + ROWS].T, row_sin[at : at + ROWS].T], 1)
-            for at in range(0, TILE, ROWS)
-        ]
-    )
-    held["row_back"] = as_left(back)
+    lines = []
+    backs = []
+    for at in range(0, TILE, ROWS):
+        high, low = halves(
+            np.concatenate([row_cos[at : at + ROWS], row_sin[at : at + ROWS]], 0)
+        )
+        lines.append(
+            np.concatenate(
+                [np.concatenate([high, high], 1), np.concatenate([low, 0 * low], 1)], 0
+            )
+        )
+        backs.append(
+            as_left(np.concatenate([row_cos[at : at + ROWS].T, row_sin[at : at + ROWS].T], 0))
+        )
+    held["row"] = np.stack(lines)
+    held["row_back"] = np.stack(backs)
     col = angles(narrow, coarse)
     col_cos = np.cos(col) / math.sqrt(BAND)
     col_sin = np.sin(col) / math.sqrt(BAND)
@@ -128,9 +133,38 @@
     out_ref[...] = packed.astype(f32) + weights
 
 
-def swap_sign(value, first_half):
-    turned = pltpu.roll(value, BAND, 1)
-    return jnp.where(first_half, -turned, turned)
+def spectrum_kernel(
+    mask_hbm, right_hbm, left_hbm, after_hbm, re_ref, im_ref, mask_ref, right_ref, left_ref, sems
+):
+    half_tile = TILE // 2
+    pairs = [(right_hbm, right_ref)]
+    for t in range(2):
+        for part in range(2):
+            rows = pl.ds(part * half_tile, half_tile)
+            pairs.append((mask_hbm.at[t, rows], mask_ref.at[t, rows]))
+    pairs.insert(3, (left_hbm, left_ref))
+    loads = [pltpu.make_async_copy(*pair, sems.at[n]) for n, pair in enumerate(pairs)]
+    for load in loads:
+        load.start()
+    loads[0].wait()
+    for t in range(2):
+        highs = []
+        lows = []
+        for part in range(2):
+            loads[1 + 3 * t + part].wait()
+            high, low = split(mask_ref[t, part * half_tile : (part + 1) * half_tile])
+            high, low = split(
+                mm(high, right_ref[0]) + mm(high, right_ref[1]) + mm(low, right_ref[0])
+            )
+            highs.append(high)
+            lows.append(low)
+        high = jnp.concatenate(highs, 0)
+        low = jnp.concatenate(lows, 0)
+        if t == 0:
+            loads[3].wait()
+        blocks = mm(left_ref[0], high) + mm(left_ref[0], low) + mm(left_ref[1], high)
+        re_ref[t] = blocks[:WIDTH, :WIDTH] - blocks[WIDTH:, WIDTH:]
+        im_ref[t] = pltpu.roll(-(blocks[WIDTH:, :WIDTH] + blocks[:WIDTH, WIDTH:]), BAND, 1)
 
 
 def place_of(number):
@@ -141,36 +175,37 @@
 
 
 def main_kernel(
-    count_ref,
-    point_ref,
-    pupil_ref,
-    mask_hbm,
-    right_hbm,
-    left_hbm,
+    point_hbm,
+    count_hbm,
+    re_hbm,
+    im_hbm,
+    pupil_hbm,
+    row_hbm,
+    col_hbm,
     dose_hbm,
     target_hbm,
     raise_hbm,
     lower_hbm,
     col_back_hbm,
+    row_back_hbm,
     fold_hbm,
-    row_hbm,
-    row_back_hbm,
-    col_hbm,
+    lines_hbm,
     out_ref,
-    mask_ref,
-    right_ref,
-    left_ref,
+    point_ref,
+    count_ref,
+    re_ref,
+    im_ref,
+    pupil_ref,
+    row_ref,
+    col_ref,
     dose_ref,
     target_ref,
     raise_ref,
     lower_ref,
     col_back_ref,
+    row_back_ref,
     fold_ref,
-    row_ref,
-    row_back_ref,
-    col_ref,
-    re_ref,
-    im_ref,
+    right_ref,
     half_ref,
     field_ref,
     total_ref,
@@ -182,59 +217,42 @@
 ):
     clip = lax.axis_index("clip")
     me = lax.axis_index("src")
-    half_tile = TILE // 2
     loads = [
         pltpu.make_async_copy(source, target, sems.at[n])
         for n, (source, target) in enumerate(
             (
-                (right_hbm, right_ref),
-                (mask_hbm.at[0, :half_tile], mask_ref.at[0, :half_tile]),
-                (mask_hbm.at[0, half_tile:], mask_ref.at[0, half_tile:]),
-                (left_hbm, left_ref),
-                (mask_hbm.at[1, :half_tile], mask_ref.at[1, :half_tile]),
-                (mask_hbm.at[1, half_tile:], mask_ref.at[1, half_tile:]),
+                (point_hbm, point_ref),
+                (re_hbm, re_ref),
+                (im_hbm, im_ref),
+                (pupil_hbm, pupil_ref),
                 (row_hbm.at[me], row_ref),
                 (col_hbm, col_ref),
                 (dose_hbm, dose_ref),
+                (raise_hbm, raise_ref),
                 (target_hbm, target_ref),
-                (raise_hbm, raise_ref),
+                (count_hbm, count_ref),
                 (lower_hbm, lower_ref),
                 (col_back_hbm, col_back_ref),
                 (row_back_hbm.at[me], row_back_ref),
                 (fold_hbm, fold_ref),
+                (lines_hbm, right_ref),
             )
         )
     ]
     for load in loads:
         load.start()
-    first_half = lax.broadcasted_iota(jnp.int32, (BAND, WIDTH), 1) < BAND
+    lane = lax.broadcasted_iota(jnp.int32, (BAND, WIDTH), 1)
+    first_half = lane < BAND
     total_ref[...] = jnp.zeros_like(total_ref)
     adj_ref[...] = jnp.zeros_like(adj_ref)
     term_ref[...] = jnp.zeros_like(term_ref)
     rows = 2 * ROWS
-    pupil_both = [jnp.concatenate([pupil_ref[n], pupil_ref[n]], 1) for n in range(2)]
-
-    loads[0].wait()
-    for t in range(2):
-        highs = []
-        lows = []
-        for part in range(2):
-            loads[1 + 3 * t + part].wait()
-            high, low = split(mask_ref[t, part * half_tile : (part + 1) * half_tile])
-            high, low = split(
-                mm(high, right_ref[0]) + mm(high, right_ref[1]) + mm(low, right_ref[0])
-            )
-            highs.append(high)
-            lows.append(low)
-        high = jnp.concatenate(highs, 0)
-        low = jnp.concatenate(lows, 0)
-        if t == 0:
-            loads[3].wait()
-        blocks = mm(left_ref[0], high) + mm(left_ref[0], low) + mm(left_ref[1], high)
-        re_ref[t] = blocks[:WIDTH, :WIDTH] - blocks[WIDTH:, WIDTH:]
-        im_ref[t] = -(blocks[WIDTH:, :WIDTH] + blocks[:WIDTH, WIDTH:])
-    loads[6].wait()
-    loads[7].wait()
+    for load in loads[:5]:
+        load.wait()
+    pupil_re, pupil_im = [jnp.concatenate([pupil_ref[n], pupil_ref[n]], 1) for n in range(2)]
+    pupil_re_odd = jnp.where(first_half, -pupil_re, pupil_re)
+    pupil_im_odd = jnp.where(first_half, -pupil_im, pupil_im)
+    odd = jnp.where(first_half[:ROWS], -1.0, 1.0).astype(f32)
 
     def weight_of(k):
         return point_ref[k >> 1, 0, 2 + (k & 1)]
@@ -246,34 +264,35 @@
         for inner in range(8):
             k = step * 8 + inner
             row_pos, col_pos = window_of(k)
-            back = (WIDTH - col_pos) & (WIDTH - 1)
-            back_half = (WIDTH + BAND - col_pos) & (WIDTH - 1)
-            held = []
+            inside = (lane >= col_pos) & (lane < col_pos + BAND)
+            highs = []
+            lows = []
             for t in range(2):
-                window = jnp.where(
-                    first_half,
-                    pltpu.roll(re_ref[t, pl.ds(row_pos, BAND), :], back, 1),
-                    pltpu.roll(im_ref[t, pl.ds(row_pos, BAND), :], back_half, 1),
+                mixed = jnp.where(
+                    inside, re_ref[t, pl.ds(row_pos, BAND), :], im_ref[t, pl.ds(row_pos, BAND), :]
                 )
-                turned = swap_sign(window, first_half)
-                pupil_re, pupil_im = pupil_both
-                high, low = split(
-                    jnp.concatenate(
-                        [
-                            pupil_re * window + pupil_im * turned,
-                            pupil_re * turned - pupil_im * window,
-                        ],
-                        0,
-                    )
-                )
-                held.append(jnp.concatenate([high, low], 0))
-            half = mm(row_ref[...], jnp.concatenate(held, 1))
-            half = half[:ROWS] + half[ROWS:]
-            half = jnp.concatenate([half[:, :WIDTH], half[:, WIDTH:]], 0)
+                window = pltpu.roll(mixed, (WIDTH - col_pos) & (WIDTH - 1), 1)
+                turned = pltpu.roll(mixed, (WIDTH + BAND - col_pos) & (WIDTH - 1), 1)
+                high, low = split(pupil_re * window + pupil_im_odd * turned)
+                highs.append(high)
+                lows.append(low)
+            both = mm(
+                row_ref[...],
+                jnp.concatenate([jnp.concatenate(highs, 1), jnp.concatenate(lows, 1)], 0),
+            )
+            both = both[:rows] + both[rows:]
+            half = jnp.concatenate(
+                [
+                    both[:ROWS, at : at + WIDTH] + odd * pltpu.roll(both[ROWS:, at : at + WIDTH], BAND, 1)
+                    for at in (0, WIDTH)
+                ],
+                0,
+            )
             half_ref[pl.ds(pl.multiple_of(k * rows, rows), rows), :] = split_cols(half)
         return carry
 
     lax.fori_loop(0, POINTS // 8, windows, 0)
+    loads[5].wait()
 
     def fields(step, carry):
         field = mm(
@@ -292,7 +311,7 @@
 
     lax.fori_loop(0, POINTS // 8, fields, 0)
 
-    for load in loads[8:]:
+    for load in loads[6:]:
         load.wait()
     intensity = mm(split_cols(total_ref[...]), raise_ref[...])
     for t in range(2):
@@ -338,23 +357,22 @@
         for inner in range(8):
             k = step * 8 + inner
             row_pos, col_pos = window_of(k)
+            inside = (lane >= col_pos) & (lane < col_pos + BAND)
             half = back_ref[pl.ds(pl.multiple_of(k * rows, rows), rows), :]
-            turned = -swap_sign(half, first_half)
-            pair = jnp.concatenate(
-                [
-                    split_rows(jnp.concatenate([half[:ROWS], turned[:ROWS]], 0)),
-                    split_rows(jnp.concatenate([half[ROWS:], turned[ROWS:]], 0)),
-                ],
-                1,
-            )
-            both = mm(row_back_ref[...], pair)
+            both = mm(
+                row_back_ref[...],
+                split_rows(jnp.concatenate([half[:ROWS], half[ROWS:]], 1)),
+            )
             for t in range(2):
-                held = both[:, t * WIDTH : (t + 1) * WIDTH]
-                spread = pupil_both[0] * held - pupil_both[1] * swap_sign(held, first_half)
-                spread_re = pltpu.roll(jnp.where(first_half, spread, 0.0), col_pos, 1)
-                spread_im = pltpu.roll(jnp.where(first_half, 0.0, spread), col_pos + BAND, 1)
-                adj_ref[t, pl.ds(row_pos, BAND), :] += spread_re
-                adj_ref[2 + t, pl.ds(row_pos, BAND), :] += spread_im
+                by_cos = both[:BAND, t * WIDTH : (t + 1) * WIDTH]
+                by_sin = both[BAND:, t * WIDTH : (t + 1) * WIDTH]
+                straight = pupil_re * by_cos - pupil_im * by_sin
+                crossed = pupil_im_odd * by_cos + pupil_re_odd * by_sin
+                spread = pltpu.roll(straight, col_pos, 1) + pltpu.roll(
+                    crossed, (col_pos + BAND) & (WIDTH - 1), 1
+                )
+                adj_ref[t, pl.ds(row_pos, BAND), :] += jnp.where(inside, spread, 0.0)
+                adj_ref[2 + t, pl.ds(row_pos, BAND), :] += jnp.where(inside, 0.0, spread)
         return carry
 
     lax.fori_loop(0, POINTS // 8, rows_back, 0)
@@ -366,7 +384,7 @@
     bottom_flat = jnp.zeros((WIDTH, WIDTH), f32)
     for t in range(2):
         adj_re = adj_ref[t]
-        adj_im = adj_ref[2 + t]
+        adj_im = pltpu.roll(adj_ref[2 + t], BAND, 1)
         high, low = split(jnp.concatenate([adj_re, adj_im], 1))
         folded = mm(high, fold_ref[...]) + mm(low, fold_ref[...])
         tops.append(folded[:, :WIDTH])
@@ -412,15 +430,6 @@
     term_ref[...] = jnp.broadcast_to(jnp.broadcast_to(sums, (8, WIDTH))[None], term_ref.shape)
 
 
-def whole(array):
-    return pl.BlockSpec(array.shape, lambda *_: (0,) * array.ndim)
-
-
-def clip_groups(clips, bits):
-    rest = [c for c in range(clips) if not c & bits]
-    return [[base | c for c in range(clips) if not c & ~bits] for base in rest]
-
-
 def per_device(
     clips, mask_field, dose_code, target, pupil, source_index, source_weight, tile_count
 ):
@@ -431,38 +440,42 @@
     mine = pl.pallas_call(
         pack_kernel,
         in_specs=[smem, smem],
-        out_shape=jax.ShapeDtypeStruct((SRC, 8, WIDTH), f32),
+        out_shape=jax.ShapeDtypeStruct((SRC, 1, WIDTH), f32),
         name="pack",
     )(source_index, source_weight)
     points = lax.all_to_all(mine, "src", 0, 0)
 
-    tables = [
-        held[n]
-        for n in (
-            "spec_right",
-            "spec_left",
-            "raise",
-            "lower",
-            "col_back",
-            "fold",
-            "row",
-            "row_back",
-            "col",
-        )
-    ]
-    stored = [mask_field, *tables[:2], dose_code, target, *tables[2:]]
-    landing = [
-        pltpu.VMEM(a.shape[1:] if n in (9, 10) else a.shape, a.dtype)
-        for n, a in enumerate(stored)
-    ]
+    roomy = pltpu.CompilerParams(vmem_limit_bytes=56 * 1024 * 1024)
+    stored = [mask_field, held["spec_right"], held["spec_left"]]
+    spec_shape = jax.ShapeDtypeStruct((2, WIDTH, WIDTH), f32)
+    spec_re, spec_im = pl.pallas_call(
+        spectrum_kernel,
+        in_specs=[hbm] * 4,
+        out_shape=[spec_shape, spec_shape],
+        scratch_shapes=[pltpu.VMEM(a.shape, a.dtype) for a in stored]
+        + [pltpu.SemaphoreType.DMA((6,))],
+        compiler_params=roomy,
+        cost_estimate=pl.CostEstimate(
+            flops=1_200_000_000, bytes_accessed=3_000_000, transcendentals=0
+        ),
+        name="spectrum",
+    )(*stored, mine)
+
+    stored = [points, tile_count, spec_re, spec_im, pupil, held["row"], held["col"]]
+    stored += [dose_code, target, held["raise"], held["lower"], held["col_back"]]
+    stored += [held["row_back"], held["fold"], held["spec_right"]]
+    landing = [pltpu.VMEM(a.shape, a.dtype) for a in stored]
+    landing[0] = pltpu.SMEM(points.shape, f32)
+    landing[1] = pltpu.SMEM(tile_count.shape, jnp.int32)
+    for n in (5, 12):
+        landing[n] = pltpu.VMEM(stored[n].shape[1:], bf16)
     blocks = pl.pallas_call(
         main_kernel,
-        in_specs=[smem, smem, whole(pupil)] + [hbm] * len(stored),
+        in_specs=[hbm] * len(stored),
+        out_specs=pl.BlockSpec(memory_space=pltpu.VMEM),
         out_shape=jax.ShapeDtypeStruct((SRC, CHUNK, WIDTH), f32),
         scratch_shapes=landing
         + [
-            pltpu.VMEM((2, WIDTH, WIDTH), f32),
-            pltpu.VMEM((2, WIDTH, WIDTH), f32),
             pltpu.VMEM((POINTS * 2 * ROWS, 3 * WIDTH), bf16),
             pltpu.VMEM((POINTS, 2 * ROWS, 2 * WIDTH), f32),
             pltpu.VMEM((2 * ROWS, WIDTH), f32),
@@ -470,22 +483,21 @@
             pltpu.VMEM((POINTS * 2 * ROWS, WIDTH), f32),
             pltpu.VMEM((4, WIDTH, WIDTH), f32),
             pltpu.VMEM((SRC, 8, WIDTH), f32),
-            pltpu.SemaphoreType.DMA((len(stored) + 3,)),
+            pltpu.SemaphoreType.DMA((len(stored),)),
         ],
-        compiler_params=pltpu.CompilerParams(vmem_limit_bytes=30 * 1024 * 1024),
+        compiler_params=roomy,
         cost_estimate=pl.CostEstimate(
             flops=3_000_000_000, bytes_accessed=5_000_000, transcendentals=300_000
         ),
         name="fields",
-    )(tile_count, points, pupil, *stored)
+    )(*stored)
 
     chunks = lax.all_to_all(blocks, "src", 0, 0)
-    near = 4 if clips == 32 else 1
     grad_mask, term = pl.pallas_call(
         image_kernel,
         out_shape=[
             jax.ShapeDtypeStruct((2, ROWS, TILE), f32),
-            jax.ShapeDtypeStruct((near, 8, WIDTH), f32),
+            jax.ShapeDtypeStruct((clips, 8, WIDTH), f32),
         ],
         compiler_params=pltpu.CompilerParams(vmem_limit_bytes=12 * 1024 * 1024),
         cost_estimate=pl.CostEstimate(
@@ -493,10 +505,7 @@
         ),
         name="image",
     )(chunks, held["image"])
-    if clips == 32:
-        term = lax.all_to_all(term, "clip", 0, 0, axis_index_groups=clip_groups(clips, 17))
-        term = jnp.broadcast_to(jnp.sum(term, 0), (8, 8, WIDTH))
-        term = lax.all_to_all(term, "clip", 0, 0, axis_index_groups=clip_groups(clips, 14))
+    term = lax.all_to_all(term, "clip", 0, 0)
     grad_source = jnp.sum(term[:, 2:4, 0], 0)
     return (grad_mask, grad_source)
 

time: 101 us -> 80.3 us (0.80)
  blocking collectives: 65.2 us -> 45.8 us
  local copies, waits for them, and re-layouts: 14.1 us -> 0.59 us
  starting transfers between devices: 0 us -> 10.2 us
  waiting for transfers between devices: 0 us -> 3.54 us
  Pallas kernels: 19.6 us -> 18.5 us
    all_to_all x3 -> x1, blocking collectives: 44 us -> 21.5 us  [per_device(): term = lax.all_to_all(term, 'clip', 0, 0)]
    unnamed x30 -> x4, local copies, waits for them, and re-layouts: 14.1 us -> 0.59 us
    all_to_all x0 -> x1, starting transfers between devices: none -> 10.2 us  [per_device(): points = lax.all_to_all(mine, 'src', 0, 0)]
    all_to_all x0 -> x1, waiting for transfers between devices: none -> 3.54 us  [per_device(): points = lax.all_to_all(mine, 'src', 0, 0)]
    all_to_all x1, blocking collectives: 21.2 us -> 24.3 us  [per_device(): chunks = lax.all_to_all(blocks, 'src', 0, 0)]
    pallas_call x1 -> x2, Pallas kernels: 17.4 us -> 16.4 us  [the longest x1 11.1 us: per_device(): pl.pallas_call(main_kernel, in_specs=[hbm] * len(stored), out_specs=pl.Bl...]
  transfers between devices with their start and end apart: 0 -> 1, of which waited for: 0 -> 1; matrix products, arithmetic and copies ran while one was open for 0% -> 0% of each run, Pallas kernels for 0% -> 7%
where the time goes in v2:
time: 80.3 us; the launch traced here: 80 us
  blocking collectives  45.8 us (57%)
  Pallas kernels  18.5 us (23%)
  starting transfers between devices  10.2 us (13%)
  waiting for transfers between devices  3.54 us (4%)
    all_to_all x1, blocking collectives, per_device(): chunks = lax.all_to_all(blocks, 'src', 0, 0)  24.3 us
    all_to_all x1, blocking collectives, per_device(): term = lax.all_to_all(term, 'clip', 0, 0)  21.5 us
    pallas_call x1, Pallas kernels, per_device(): pl.pallas_call(main_kernel, in_specs=[hbm] * len(stored), out_specs=pl.Bl...  11.1 us
    all_to_all x1, starting transfers between devices, per_device(): points = lax.all_to_all(mine, 'src', 0, 0)  10.2 us
    pallas_call x1, Pallas kernels, per_device(): pl.pallas_call(spectrum_kernel, in_specs=[hbm] * 4, out_shape=[spec_shape...  5.27 us
    all_to_all x1, waiting for transfers between devices, per_device(): points = lax.all_to_all(mine, 'src', 0, 0)  3.54 us
  transfers between devices with their start and end apart: 1, of which 1 were waited for; matrix products, arithmetic and copies ran while one was open for 0% of the time, Pallas kernels for 7%

profile of v2, /device:TPU:1, one launch (start us, length us, event | category | flops | bytes accessed | tf_op | source)
XLA Modules:
  0.0 80.0 jit_solution(4420930864675113780)
XLA Ops:
  0.6 1.3 %pack.1.after_hbm = f32[16,1,128]{2,1,0:T(1,128)} custom-call(s32[2]{0:T(128)} %index_ref.1, f32[2]{0:T(128)} %weight_ref.1), custom_call_target="tpu_custom_call" | custom-call | tf_op jit(solution)/shard_map/pack/pallas_call | solution.py:440
  1.9 10.2 %all-to-all-start = ((f32[16,1,128]{2,1,0:T(1,128)}), f32[16,1,128]{2,1,0:T(1,128)S(1)}, u32[]{:S(2)}, u32[]{:S(2)}) async-start(f32[16,1,128]{2,1,0:T(1,128)} %pack.1.after_hbm), calls=%async_computation | async-start | bytes 16384 | tf_op jit(solution)/shard_map/all_to_all | solution.py:446
  12.1 5.3 %spectrum.1 = (f32[2,128,128]{2,1,0:T(8,128)}, f32[2,128,128]{2,1,0:T(8,128)}) custom-call(f32[2,512,512]{2,1,0:T(8,128)} %mask_hbm.1, bf16[2,512,256]{2,1,0:T(8,128)(2,1)} %constant.22.clone.right_hbm.lines_hbm, bf16[2,256,512]{2,1,0:T(8,128)(2,1)} %constant.23.clone.left_hbm, f32[16,1,128]{2,1,0:T(1,128)} %pack.1.after_hbm), custom_call_target="tpu_custom_call" | custom-call | flops 1200000000 | bytes 3000000 | tf_op jit(solution)/shard_map/spectrum/pallas_call | solution.py:451
  17.4 3.5 %all-to-all-done.point_hbm = f32[16,1,128]{2,1,0:T(1,128)S(1)} async-done(((f32[16,1,128]{2,1,0:T(1,128)}), f32[16,1,128]{2,1,0:T(1,128)S(1)}, u32[]{:S(2)}, u32[]{:S(2)}) %all-to-all-start) | async-done | bytes 8224 | tf_op jit(solution)/shard_map/all_to_all | solution.py:446
  20.9 0.0 copy-start.1
  20.9 0.6 copy-done.1
  21.5 0.0 copy-start
  21.5 11.1 %fields.1 = f32[16,72,128]{2,1,0:T(8,128)} custom-call(f32[16,1,128]{2,1,0:T(1,128)} %copy-done.1, s32[16]{0:T(128)} %count_hbm.1, f32[2,128,128]{2,1,0:T(8,128)} %get-tuple-element.6.re_hbm, f32[2,128,128]{2,1,0:T(8,128)} %get-tuple-element.7.im_hbm, f32[2,64,64]{2,1,0:T(8,128)} %pupil_hbm.1, bf16[16,128,128]{2,1,0:T(8,128)(2,1)} %constant.24.clone.row_hbm, ...), custom_call_target="tpu_custom_call" | custom-call | flops 3000000000 | bytes 5000000 | tf_op jit(solution)/shard_map/fields/pallas_call | solution.py:472
  32.7 24.3 %all_to_all.15.chunk_ref = f32[16,72,128]{2,1,0:T(8,128)S(1)} all-to-all(f32[16,72,128]{2,1,0:T(8,128)} %fields.1), channel_id=1, replica_groups=mesh['clip'=32,'src'=16] {'src'}, dimensions={0} | all-to-all | bytes 1179648 | tf_op jit(solution)/shard_map/all_to_all | solution.py:495
  57.0 0.0 copy-done
  57.0 0.9 %image.1 = (f32[2,32,512]{2,1,0:T(8,128)}, f32[32,8,128]{2,1,0:T(8,128)S(1)}) custom-call(f32[16,72,128]{2,1,0:T(8,128)S(1)} %all_to_all.15.chunk_ref, bf16[384,512]{1,0:T(8,128)(2,1)S(1)} %copy-done), custom_call_target="tpu_custom_call" | custom-call | flops 100000000 | bytes 1000000 | tf_op jit(solution)/shard_map/image/pallas_call | solution.py:496
  57.8 21.5 %all_to_all.16 = f32[32,8,128]{2,1,0:T(8,128)S(1)} all-to-all(f32[32,8,128]{2,1,0:T(8,128)S(1)} %get-tuple-element.9), channel_id=1, replica_groups=mesh['clip'=32,'src'=16] {'clip'}, dimensions={0} | all-to-all | bytes 262144 | tf_op jit(solution)/shard_map/all_to_all | solution.py:508
  79.3 0.7 slice_reduce_fusion
Async XLA Ops:
  1.9 19.0 %all-to-all-start = ((f32[16,1,128]{2,1,0:T(1,128)}), f32[16,1,128]{2,1,0:T(1,128)S(1)}, u32[]{:S(2)}, u32[]{:S(2)}) async-start(f32[16,1,128]{2,1,0:T(1,128)} %pack.1.after_hbm), calls=%async_computation | async-start | bytes 16384 | tf_op jit(solution)/shard_map/all_to_all | solution.py:446
  20.9 0.6 copy-start.1
  21.5 35.4 %copy-start = (bf16[384,512]{1,0:T(8,128)(2,1)S(1)}, bf16[384,512]{1,0:T(8,128)(2,1)}, u32[]{:S(2)}) copy-start(bf16[384,512]{1,0:T(8,128)(2,1)} %constant.31.clone.table_ref) | copy-start | bytes 1179652

commit v3 on v2

--- a/solution.py
+++ b/solution.py
@@ -126,42 +126,25 @@
     return jnp.dot(left, right, preferred_element_type=f32)
 
 
-def pack_kernel(index_ref, weight_ref, out_ref):
+def pack_kernel(index_any, weight_any, out_ref, index_ref, weight_ref, sems):
+    loads = [
+        pltpu.make_async_copy(index_any, index_ref, sems.at[0]),
+        pltpu.make_async_copy(weight_any, weight_ref, sems.at[1]),
+    ]
+    for load in loads:
+        load.start()
     lane = lax.broadcasted_iota(jnp.int32, out_ref.shape, 2)
+    for load in loads:
+        load.wait()
     packed = jnp.where(lane == 0, index_ref[0], jnp.where(lane == 1, index_ref[1], 0))
     weights = jnp.where(lane == 2, weight_ref[0], jnp.where(lane == 3, weight_ref[1], 0.0))
     out_ref[...] = packed.astype(f32) + weights
 
 
-def spectrum_kernel(
-    mask_hbm, right_hbm, left_hbm, after_hbm, re_ref, im_ref, mask_ref, right_ref, left_ref, sems
-):
-    half_tile = TILE // 2
-    pairs = [(right_hbm, right_ref)]
+def spectrum_kernel(mask_ref, right_ref, left_ref, after_hbm, re_ref, im_ref):
     for t in range(2):
-        for part in range(2):
-            rows = pl.ds(part * half_tile, half_tile)
-            pairs.append((mask_hbm.at[t, rows], mask_ref.at[t, rows]))
-    pairs.insert(3, (left_hbm, left_ref))
-    loads = [pltpu.make_async_copy(*pair, sems.at[n]) for n, pair in enumerate(pairs)]
-    for load in loads:
-        load.start()
-    loads[0].wait()
-    for t in range(2):
-        highs = []
-        lows = []
-        for part in range(2):
-            loads[1 + 3 * t + part].wait()
-            high, low = split(mask_ref[t, part * half_tile : (part + 1) * half_tile])
-            high, low = split(
-                mm(high, right_ref[0]) + mm(high, right_ref[1]) + mm(low, right_ref[0])
-            )
-            highs.append(high)
-            lows.append(low)
-        high = jnp.concatenate(highs, 0)
-        low = jnp.concatenate(lows, 0)
-        if t == 0:
-            loads[3].wait()
+        high, low = split(mask_ref[t])
+        high, low = split(mm(high, right_ref[0]) + mm(high, right_ref[1]) + mm(low, right_ref[0]))
         blocks = mm(left_ref[0], high) + mm(left_ref[0], low) + mm(left_ref[1], high)
         re_ref[t] = blocks[:WIDTH, :WIDTH] - blocks[WIDTH:, WIDTH:]
         im_ref[t] = pltpu.roll(-(blocks[WIDTH:, :WIDTH] + blocks[:WIDTH, WIDTH:]), BAND, 1)
@@ -175,24 +158,8 @@
 
 
 def main_kernel(
-    point_hbm,
-    count_hbm,
-    re_hbm,
-    im_hbm,
-    pupil_hbm,
-    row_hbm,
-    col_hbm,
-    dose_hbm,
-    target_hbm,
-    raise_hbm,
-    lower_hbm,
-    col_back_hbm,
-    row_back_hbm,
-    fold_hbm,
-    lines_hbm,
-    out_ref,
-    point_ref,
-    count_ref,
+    point_any,
+    count_any,
     re_ref,
     im_ref,
     pupil_ref,
@@ -206,6 +173,9 @@
     row_back_ref,
     fold_ref,
     right_ref,
+    out_ref,
+    point_ref,
+    count_ref,
     half_ref,
     field_ref,
     total_ref,
@@ -218,26 +188,8 @@
     clip = lax.axis_index("clip")
     me = lax.axis_index("src")
     loads = [
-        pltpu.make_async_copy(source, target, sems.at[n])
-        for n, (source, target) in enumerate(
-            (
-                (point_hbm, point_ref),
-                (re_hbm, re_ref),
-                (im_hbm, im_ref),
-                (pupil_hbm, pupil_ref),
-                (row_hbm.at[me], row_ref),
-                (col_hbm, col_ref),
-                (dose_hbm, dose_ref),
-                (raise_hbm, raise_ref),
-                (target_hbm, target_ref),
-                (count_hbm, count_ref),
-                (lower_hbm, lower_ref),
-                (col_back_hbm, col_back_ref),
-                (row_back_hbm.at[me], row_back_ref),
-                (fold_hbm, fold_ref),
-                (lines_hbm, right_ref),
-            )
-        )
+        pltpu.make_async_copy(point_any, point_ref, sems.at[0]),
+        pltpu.make_async_copy(count_any, count_ref, sems.at[1]),
     ]
     for load in loads:
         load.start()
@@ -247,12 +199,12 @@
     adj_ref[...] = jnp.zeros_like(adj_ref)
     term_ref[...] = jnp.zeros_like(term_ref)
     rows = 2 * ROWS
-    for load in loads[:5]:
-        load.wait()
     pupil_re, pupil_im = [jnp.concatenate([pupil_ref[n], pupil_ref[n]], 1) for n in range(2)]
     pupil_re_odd = jnp.where(first_half, -pupil_re, pupil_re)
     pupil_im_odd = jnp.where(first_half, -pupil_im, pupil_im)
     odd = jnp.where(first_half[:ROWS], -1.0, 1.0).astype(f32)
+    for load in loads:
+        load.wait()
 
     def weight_of(k):
         return point_ref[k >> 1, 0, 2 + (k & 1)]
@@ -260,7 +212,7 @@
     def window_of(k):
         return place_of(point_ref[k >> 1, 0, k & 1])
 
-    def windows(step, carry):
+    def windows(step):
         for inner in range(8):
             k = step * 8 + inner
             row_pos, col_pos = window_of(k)
@@ -277,7 +229,7 @@
                 highs.append(high)
                 lows.append(low)
             both = mm(
-                row_ref[...],
+                row_ref[me],
                 jnp.concatenate([jnp.concatenate(highs, 1), jnp.concatenate(lows, 1)], 0),
             )
             both = both[:rows] + both[rows:]
@@ -289,12 +241,8 @@
                 0,
             )
             half_ref[pl.ds(pl.multiple_of(k * rows, rows), rows), :] = split_cols(half)
-        return carry
-
-    lax.fori_loop(0, POINTS // 8, windows, 0)
-    loads[5].wait()
-
-    def fields(step, carry):
+
+    def fields(step):
         field = mm(
             half_ref[pl.ds(pl.multiple_of(step * 8 * rows, 8 * rows), 8 * rows), :], col_ref[...]
         )
@@ -307,12 +255,19 @@
                 one[:, :WIDTH] * one[:, :WIDTH] + one[:, WIDTH:] * one[:, WIDTH:]
             )
         total_ref[...] = total
-        return carry
-
-    lax.fori_loop(0, POINTS // 8, fields, 0)
-
-    for load in loads[6:]:
-        load.wait()
+
+    def in_turn(first, second):
+        def both(step, carry):
+            second(step - 1)
+            first(step)
+            return carry
+
+        first(0)
+        lax.fori_loop(1, POINTS // 8, both, 0)
+        second(POINTS // 8 - 1)
+
+    in_turn(windows, fields)
+
     intensity = mm(split_cols(total_ref[...]), raise_ref[...])
     for t in range(2):
         slot = (clip & 1) * 2 + t
@@ -327,7 +282,7 @@
         slope_ref[t * ROWS : (t + 1) * ROWS] = (8.0 * live) * slope
     slope_ref[:, :WIDTH] = mm(split_cols(slope_ref[...]), lower_ref[...])
 
-    def columns_back(step, carry):
+    def columns_back(step):
         slope = slope_ref[:, :WIDTH]
         highs = []
         lows = []
@@ -349,18 +304,15 @@
         back_ref[pl.ds(pl.multiple_of(step * 8 * rows, 8 * rows), 8 * rows), :] = (
             half[:, :WIDTH] + half[:, WIDTH:] + rest
         )
-        return carry
-
-    lax.fori_loop(0, POINTS // 8, columns_back, 0)
-
-    def rows_back(step, carry):
+
+    def rows_back(step):
         for inner in range(8):
             k = step * 8 + inner
             row_pos, col_pos = window_of(k)
             inside = (lane >= col_pos) & (lane < col_pos + BAND)
             half = back_ref[pl.ds(pl.multiple_of(k * rows, rows), rows), :]
             both = mm(
-                row_back_ref[...],
+                row_back_ref[me],
                 split_rows(jnp.concatenate([half[:ROWS], half[ROWS:]], 1)),
             )
             for t in range(2):
@@ -373,9 +325,8 @@
                 )
                 adj_ref[t, pl.ds(row_pos, BAND), :] += jnp.where(inside, spread, 0.0)
                 adj_ref[2 + t, pl.ds(row_pos, BAND), :] += jnp.where(inside, 0.0, spread)
-        return carry
-
-    lax.fori_loop(0, POINTS // 8, rows_back, 0)
+
+    in_turn(columns_back, rows_back)
 
     lane = lax.broadcasted_iota(jnp.int32, (WIDTH, WIDTH), 1)
     tops = []
@@ -434,48 +385,48 @@
     clips, mask_field, dose_code, target, pupil, source_index, source_weight, tile_count
 ):
     held = {name: jnp.asarray(table) for name, table in constants().items()}
-    smem = pl.BlockSpec(memory_space=pltpu.SMEM)
-    hbm = pl.BlockSpec(memory_space=pltpu.HBM)
+    vmem = pl.BlockSpec(memory_space=pltpu.VMEM)
+    free = pl.BlockSpec(memory_space=pl.ANY)
 
     mine = pl.pallas_call(
         pack_kernel,
-        in_specs=[smem, smem],
+        in_specs=[free, free],
         out_shape=jax.ShapeDtypeStruct((SRC, 1, WIDTH), f32),
+        scratch_shapes=[
+            pltpu.SMEM(source_index.shape, jnp.int32),
+            pltpu.SMEM(source_weight.shape, f32),
+            pltpu.SemaphoreType.DMA((2,)),
+        ],
+        compiler_params=pltpu.CompilerParams(vmem_limit_bytes=2 * 1024 * 1024),
+        cost_estimate=pl.CostEstimate(
+            flops=8_000_000_000, bytes_accessed=20_000_000, transcendentals=0
+        ),
         name="pack",
     )(source_index, source_weight)
     points = lax.all_to_all(mine, "src", 0, 0)
 
-    roomy = pltpu.CompilerParams(vmem_limit_bytes=56 * 1024 * 1024)
-    stored = [mask_field, held["spec_right"], held["spec_left"]]
     spec_shape = jax.ShapeDtypeStruct((2, WIDTH, WIDTH), f32)
     spec_re, spec_im = pl.pallas_call(
         spectrum_kernel,
-        in_specs=[hbm] * 4,
+        in_specs=[vmem] * 3 + [free],
         out_shape=[spec_shape, spec_shape],
-        scratch_shapes=[pltpu.VMEM(a.shape, a.dtype) for a in stored]
-        + [pltpu.SemaphoreType.DMA((6,))],
-        compiler_params=roomy,
+        compiler_params=pltpu.CompilerParams(vmem_limit_bytes=20 * 1024 * 1024),
         cost_estimate=pl.CostEstimate(
-            flops=1_200_000_000, bytes_accessed=3_000_000, transcendentals=0
+            flops=2_400_000_000, bytes_accessed=3_000_000, transcendentals=0
         ),
         name="spectrum",
-    )(*stored, mine)
-
-    stored = [points, tile_count, spec_re, spec_im, pupil, held["row"], held["col"]]
+    )(mask_field, held["spec_right"], held["spec_left"], mine)
+
+    stored = [spec_re, spec_im, pupil, held["row"], held["col"]]
     stored += [dose_code, target, held["raise"], held["lower"], held["col_back"]]
     stored += [held["row_back"], held["fold"], held["spec_right"]]
-    landing = [pltpu.VMEM(a.shape, a.dtype) for a in stored]
-    landing[0] = pltpu.SMEM(points.shape, f32)
-    landing[1] = pltpu.SMEM(tile_count.shape, jnp.int32)
-    for n in (5, 12):
-        landing[n] = pltpu.VMEM(stored[n].shape[1:], bf16)
     blocks = pl.pallas_call(
         main_kernel,
-        in_specs=[hbm] * len(stored),
-        out_specs=pl.BlockSpec(memory_space=pltpu.VMEM),
+        in_specs=[free] * 2 + [vmem] * len(stored),
         out_shape=jax.ShapeDtypeStruct((SRC, CHUNK, WIDTH), f32),
-        scratch_shapes=landing
-        + [
+        scratch_shapes=[
+            pltpu.SMEM(points.shape, f32),
+            pltpu.SMEM(tile_count.shape, jnp.int32),
             pltpu.VMEM((POINTS * 2 * ROWS, 3 * WIDTH), bf16),
             pltpu.VMEM((POINTS, 2 * ROWS, 2 * WIDTH), f32),
             pltpu.VMEM((2 * ROWS, WIDTH), f32),
@@ -483,14 +434,14 @@
             pltpu.VMEM((POINTS * 2 * ROWS, WIDTH), f32),
             pltpu.VMEM((4, WIDTH, WIDTH), f32),
             pltpu.VMEM((SRC, 8, WIDTH), f32),
-            pltpu.SemaphoreType.DMA((len(stored),)),
+            pltpu.SemaphoreType.DMA((2,)),
         ],
-        compiler_params=roomy,
+        compiler_params=pltpu.CompilerParams(vmem_limit_bytes=28 * 1024 * 1024),
         cost_estimate=pl.CostEstimate(
-            flops=3_000_000_000, bytes_accessed=5_000_000, transcendentals=300_000
+            flops=8_000_000_000, bytes_accessed=5_000_000, transcendentals=300_000
         ),
         name="fields",
-    )(*stored)
+    )(points, tile_count, *stored)
 
     chunks = lax.all_to_all(blocks, "src", 0, 0)
     grad_mask, term = pl.pallas_call(

time: 80.3 us -> 87.8 us (1.093)
  local copies, waits for them, and re-layouts: 0.59 us -> 13.6 us
  Pallas kernels: 18.5 us -> 12.8 us
  waiting for transfers between devices: 3.54 us -> 2.63 us
    unnamed x4 -> x44, local copies, waits for them, and re-layouts: 0.59 us -> 13.6 us
    pallas_call x3, Pallas kernels: 17.7 us -> 12 us  [the longest x1 8.04 us: per_device(): pl.pallas_call(main_kernel, in_specs=[free] * 2 + [vmem] * len(stored), o...]
    all_to_all x1, waiting for transfers between devices: 3.54 us -> 2.63 us  [per_device(): points = lax.all_to_all(mine, 'src', 0, 0)]
  transfers between devices with their start and end apart: 1 -> 1, of which waited for: 1 -> 1; matrix products, arithmetic and copies ran while one was open for 0% -> 0% of each run, Pallas kernels for 7% -> 3%
where the time goes in v3:
time: 87.8 us; the launch traced here: 87.1 us
  blocking collectives  46.5 us (53%)
  local copies, waits for them, and re-layouts  13.6 us (15%)
  Pallas kernels  12.8 us (15%)
  starting transfers between devices  10.2 us (12%)
  waiting for transfers between devices  2.63 us (3%)
    all_to_all x1, blocking collectives, per_device(): chunks = lax.all_to_all(blocks, 'src', 0, 0)  25 us
    all_to_all x1, blocking collectives, per_device(): term = lax.all_to_all(term, 'clip', 0, 0)  21.5 us
    unnamed x44, local copies, waits for them, and re-layouts  13.6 us
    all_to_all x1, starting transfers between devices, per_device(): points = lax.all_to_all(mine, 'src', 0, 0)  10.2 us
    pallas_call x1, Pallas kernels, per_device(): pl.pallas_call(main_kernel, in_specs=[free] * 2 + [vmem] * len(stored), o...  8.04 us
    pallas_call x1, Pallas kernels, per_device(): pl.pallas_call(spectrum_kernel, in_specs=[vmem] * 3 + [free], out_shape=[...  2.76 us
    all_to_all x1, waiting for transfers between devices, per_device(): points = lax.all_to_all(mine, 'src', 0, 0)  2.63 us
  transfers between devices with their start and end apart: 1, of which 1 were waited for; matrix products, arithmetic and copies ran while one was open for 0% of the time, Pallas kernels for 3%

profile of v3, /device:TPU:1, one launch (start us, length us, event | category | flops | bytes accessed | tf_op | source)
XLA Modules:
  0.0 87.1 jit_solution(12101114344365191252)
XLA Ops:
  0.6 0.0 copy-start.1
  0.6 0.0 copy-start.5
  0.6 0.8 copy-done.5
  1.4 0.7 copy-done.6
  2.1 1.2 %pack.1.after_hbm = f32[16,1,128]{2,1,0:T(1,128)} custom-call(s32[2]{0:T(128)S(1)} %copy-done.5, f32[2]{0:T(128)S(1)} %copy-done.6), custom_call_target="tpu_custom_call" | custom-call | flops 8000000000 | bytes 20000000 | tf_op jit(solution)/shard_map/pack/pallas_call | solution.py:391
  3.3 10.2 %all-to-all-start = ((f32[16,1,128]{2,1,0:T(1,128)}), f32[16,1,128]{2,1,0:T(1,128)S(1)}, u32[]{:S(2)}, u32[]{:S(2)}) async-start(f32[16,1,128]{2,1,0:T(1,128)} %pack.1.after_hbm), calls=%async_computation | async-start | bytes 16384 | tf_op jit(solution)/shard_map/all_to_all | solution.py:406
  13.5 0.0 copy-done.1
  13.5 0.0 copy-start.8
  13.5 1.0 %copy-done.8 = bf16[2,512,256]{2,1,0:T(8,128)(2,1)S(1)} copy-done((bf16[2,512,256]{2,1,0:T(8,128)(2,1)S(1)}, bf16[2,512,256]{2,1,0:T(8,128)(2,1)}, u32[]{:S(2)}) %copy-start.8) | copy-done | bytes 524312
  14.6 1.0 %copy-done.12 = bf16[2,256,512]{2,1,0:T(8,128)(2,1)S(1)} copy-done((bf16[2,256,512]{2,1,0:T(8,128)(2,1)S(1)}, bf16[2,256,512]{2,1,0:T(8,128)(2,1)}, u32[]{:S(2)}) %copy-start.12) | copy-done | bytes 524312
  15.6 0.0 copy-start.15
  15.6 2.8 %spectrum.1 = (f32[2,128,128]{2,1,0:T(8,128)S(1)}, f32[2,128,128]{2,1,0:T(8,128)S(1)}) custom-call(f32[2,512,512]{2,1,0:T(8,128)S(1)} %copy-done.1, bf16[2,512,256]{2,1,0:T(8,128)(2,1)S(1)} %copy-done.8, bf16[2,256,512]{2,1,0:T(8,128)(2,1)S(1)} %copy-done.12, f32[16,1,128]{2,1,0:T(1,128)} %pack.1.after_hbm), custom_call_target="tpu_custom_call" | custom-call | flops 2400000000 | bytes 3000000 | tf_op jit(solution)/shard_map/spectrum/pallas_call | solution.py:409
  18.4 0.0 copy-start.18
  18.4 0.6 copy-done.18
  19.0 0.6 copy-done.20
  19.7 2.6 %all-to-all-done.point_any = f32[16,1,128]{2,1,0:T(1,128)S(1)} async-done(((f32[16,1,128]{2,1,0:T(1,128)}), f32[16,1,128]{2,1,0:T(1,128)S(1)}, u32[]{:S(2)}, u32[]{:S(2)}) %all-to-all-start) | async-done | bytes 8224 | tf_op jit(solution)/shard_map/all_to_all | solution.py:406
  22.3 0.0 copy-done.3
  22.4 0.0 copy-start.9
  22.4 1.0 %copy-done.9 = bf16[2,512,256]{2,1,0:T(8,128)(2,1)S(1)} copy-done((bf16[2,512,256]{2,1,0:T(8,128)(2,1)S(1)}, bf16[2,512,256]{2,1,0:T(8,128)(2,1)}, u32[]{:S(2)}) %copy-start.9) | copy-done | bytes 524312
  23.4 1.0 %copy-done.10 = bf16[16,128,96]{2,1,0:T(8,128)(2,1)S(1)} copy-done((bf16[16,128,96]{2,1,0:T(8,128)(2,1)S(1)}, bf16[16,128,96]{2,1,0:T(8,128)(2,1)}, u32[]{:S(2)}) %copy-start.10) | copy-done | bytes 393240
  24.4 1.0 %copy-done.11 = bf16[16,128,128]{2,1,0:T(8,128)(2,1)S(1)} copy-done((bf16[16,128,128]{2,1,0:T(8,128)(2,1)S(1)}, bf16[16,128,128]{2,1,0:T(8,128)(2,1)}, u32[]{:S(2)}) %copy-start.11) | copy-done | bytes 524312
  25.5 1.0 %copy-done.13 = bf16[1536,128]{1,0:T(8,128)(2,1)S(1)} copy-done((bf16[1536,128]{1,0:T(8,128)(2,1)S(1)}, bf16[1536,128]{1,0:T(8,128)(2,1)}, u32[]{:S(2)}) %copy-start.13) | copy-done | bytes 393240
  26.5 1.0 %copy-done.14 = bf16[384,512]{1,0:T(8,128)(2,1)S(1)} copy-done((bf16[384,512]{1,0:T(8,128)(2,1)S(1)}, bf16[384,512]{1,0:T(8,128)(2,1)}, u32[]{:S(2)}) %copy-start.14) | copy-done | bytes 393240
  27.5 0.9 %copy-done.16 = bf16[256,256]{1,0:T(8,128)(2,1)S(1)} copy-done((bf16[256,256]{1,0:T(8,128)(2,1)S(1)}, bf16[256,256]{1,0:T(8,128)(2,1)}, u32[]{:S(2)}) %copy-start.16) | copy-done | bytes 131096
  28.4 0.9 %copy-done.17 = bf16[256,256]{1,0:T(8,128)(2,1)S(1)} copy-done((bf16[256,256]{1,0:T(8,128)(2,1)S(1)}, bf16[256,256]{1,0:T(8,128)(2,1)}, u32[]{:S(2)}) %copy-start.17) | copy-done | bytes 131096
  29.3 0.9 %copy-done.19 = f32[2,128,128]{2,1,0:T(8,128)S(1)} copy-done((f32[2,128,128]{2,1,0:T(8,128)S(1)}, f32[2,128,128]{2,1,0:T(8,128)}, u32[]{:S(2)}) %copy-start.19) | copy-done | bytes 131096
  30.2 0.9 %copy-done.21 = f32[2,128,128]{2,1,0:T(8,128)S(1)} copy-done((f32[2,128,128]{2,1,0:T(8,128)S(1)}, f32[2,128,128]{2,1,0:T(8,128)}, u32[]{:S(2)}) %copy-start.21) | copy-done | bytes 131096
  31.1 8.0 %fields.1 = f32[16,72,128]{2,1,0:T(8,128)S(1)} custom-call(f32[16,1,128]{2,1,0:T(1,128)S(1)} %all-to-all-done.point_any, s32[16]{0:T(128)S(1)} %copy-done.7, f32[2,128,128]{2,1,0:T(8,128)S(1)} %copy-done.19, f32[2,128,128]{2,1,0:T(8,128)S(1)} %copy-done.21, f32[2,64,64]{2,1,0:T(8,128)S(1)} %copy-done.4, bf16[16,128,128]{2,1,0:T(8,128)(2,1)S(1)} %copy-done.11, ...), custom_call_target="tpu_custom_call" | custom-call | flops 8000000000 | bytes 5000000 | tf_op jit(solution)/shard_map/fields/pallas_call | solution.py:423
  39.1 25.0 %all_to_all.15.chunk_ref = f32[16,72,128]{2,1,0:T(8,128)S(1)} all-to-all(f32[16,72,128]{2,1,0:T(8,128)S(1)} %fields.1), channel_id=1, replica_groups=mesh['clip'=32,'src'=16] {'src'}, dimensions={0} | all-to-all | bytes 1179648 | tf_op jit(solution)/shard_map/all_to_all | solution.py:446
  64.1 0.9 image.1
  65.0 21.5 %all_to_all.16 = f32[32,8,128]{2,1,0:T(8,128)S(1)} all-to-all(f32[32,8,128]{2,1,0:T(8,128)S(1)} %get-tuple-element.9), channel_id=1, replica_groups=mesh['clip'=32,'src'=16] {'clip'}, dimensions={0} | all-to-all | bytes 262144 | tf_op jit(solution)/shard_map/all_to_all | solution.py:459
  86.5 0.7 slice_reduce_fusion
  (21 shorter events, 0.0 us)
Async XLA Ops:
  0.6 12.9 %copy-start.1 = (f32[2,512,512]{2,1,0:T(8,128)S(1)}, f32[2,512,512]{2,1,0:T(8,128)}, u32[]{:S(2)}) copy-start(f32[2,512,512]{2,1,0:T(8,128)} %mask_ref.1) | copy-start | bytes 6291460
  0.6 0.8 copy-start.5
  1.4 0.7 copy-start.6
  3.3 19.0 %all-to-all-start = ((f32[16,1,128]{2,1,0:T(1,128)}), f32[16,1,128]{2,1,0:T(1,128)S(1)}, u32[]{:S(2)}, u32[]{:S(2)}) async-start(f32[16,1,128]{2,1,0:T(1,128)} %pack.1.after_hbm), calls=%async_computation | async-start | bytes 16384 | tf_op jit(solution)/shard_map/all_to_all | solution.py:406
  13.5 1.0 %copy-start.8 = (bf16[2,512,256]{2,1,0:T(8,128)(2,1)S(1)}, bf16[2,512,256]{2,1,0:T(8,128)(2,1)}, u32[]{:S(2)}) copy-start(bf16[2,512,256]{2,1,0:T(8,128)(2,1)} %constant.22.clone.right_ref) | copy-start | bytes 1572868
  14.6 1.0 %copy-start.12 = (bf16[2,256,512]{2,1,0:T(8,128)(2,1)S(1)}, bf16[2,256,512]{2,1,0:T(8,128)(2,1)}, u32[]{:S(2)}) copy-start(bf16[2,256,512]{2,1,0:T(8,128)(2,1)} %constant.23.clone.left_ref) | copy-start | bytes 1572868
  15.6 6.7 %copy-start.2 = (s32[2,8,32,512]{3,2,1,0:T(8,128)S(1)}, s32[2,8,32,512]{3,2,1,0:T(8,128)}, u32[]{:S(2)}) copy-start(s32[2,8,32,512]{3,2,1,0:T(8,128)} %dose_ref.1) | copy-start | bytes 3145732
  15.6 6.7 %copy-start.3 = (f32[2,32,512]{2,1,0:T(8,128)S(1)}, f32[2,32,512]{2,1,0:T(8,128)}, u32[]{:S(2)}) copy-start(f32[2,32,512]{2,1,0:T(8,128)} %target_ref.1) | copy-start | bytes 393220
  15.6 6.7 %copy-start.4 = (f32[2,64,64]{2,1,0:T(8,128)S(1)}, f32[2,64,64]{2,1,0:T(8,128)}, u32[]{:S(2)}) copy-start(f32[2,64,64]{2,1,0:T(8,128)} %pupil_ref.1) | copy-start | bytes 98308
  15.6 6.7 %copy-start.7 = (s32[16]{0:T(128)S(1)}, s32[16]{0:T(128)}, u32[]{:S(2)}) copy-start(s32[16]{0:T(128)} %count_any.1) | copy-start | bytes 196
  15.6 6.7 %copy-start.15 = (bf16[384,256]{1,0:T(8,128)(2,1)S(1)}, bf16[384,256]{1,0:T(8,128)(2,1)}, u32[]{:S(2)}) copy-start(bf16[384,256]{1,0:T(8,128)(2,1)} %constant.26.clone.col_ref) | copy-start | bytes 589828
  18.4 0.7 copy-start.18
  19.0 0.7 copy-start.20
  22.4 1.0 %copy-start.9 = (bf16[2,512,256]{2,1,0:T(8,128)(2,1)S(1)}, bf16[2,512,256]{2,1,0:T(8,128)(2,1)}, u32[]{:S(2)}) copy-start(bf16[2,512,256]{2,1,0:T(8,128)(2,1)} %constant.22.clone.right_ref) | copy-start | bytes 1572868
  23.4 1.0 %copy-start.10 = (bf16[16,128,96]{2,1,0:T(8,128)(2,1)S(1)}, bf16[16,128,96]{2,1,0:T(8,128)(2,1)}, u32[]{:S(2)}) copy-start(bf16[16,128,96]{2,1,0:T(8,128)(2,1)} %constant.25.clone.row_back_ref) | copy-start | bytes 1179652
  24.4 1.0 %copy-start.11 = (bf16[16,128,128]{2,1,0:T(8,128)(2,1)S(1)}, bf16[16,128,128]{2,1,0:T(8,128)(2,1)}, u32[]{:S(2)}) copy-start(bf16[16,128,128]{2,1,0:T(8,128)(2,1)} %constant.24.clone.row_ref) | copy-start | bytes 1572868
  25.5 1.0 %copy-start.13 = (bf16[1536,128]{1,0:T(8,128)(2,1)S(1)}, bf16[1536,128]{1,0:T(8,128)(2,1)}, u32[]{:S(2)}) copy-start(bf16[1536,128]{1,0:T(8,128)(2,1)} %constant.29.clone.lower_ref) | copy-start | bytes 1179652
  26.5 1.0 %copy-start.14 = (bf16[384,512]{1,0:T(8,128)(2,1)S(1)}, bf16[384,512]{1,0:T(8,128)(2,1)}, u32[]{:S(2)}) copy-start(bf16[384,512]{1,0:T(8,128)(2,1)} %constant.28.clone.raise_ref) | copy-start | bytes 1179652
  27.5 0.9 %copy-start.16 = (bf16[256,256]{1,0:T(8,128)(2,1)S(1)}, bf16[256,256]{1,0:T(8,128)(2,1)}, u32[]{:S(2)}) copy-start(bf16[256,256]{1,0:T(8,128)(2,1)} %constant.30.clone.fold_ref) | copy-start | bytes 393220
  28.4 0.9 %copy-start.17 = (bf16[256,256]{1,0:T(8,128)(2,1)S(1)}, bf16[256,256]{1,0:T(8,128)(2,1)}, u32[]{:S(2)}) copy-start(bf16[256,256]{1,0:T(8,128)(2,1)} %constant.27.clone.col_back_ref) | copy-start | bytes 393220
  29.3 0.9 %copy-start.19 = (f32[2,128,128]{2,1,0:T(8,128)S(1)}, f32[2,128,128]{2,1,0:T(8,128)}, u32[]{:S(2)}) copy-start(f32[2,128,128]{2,1,0:T(8,128)} %copy-done.18) | copy-start | bytes 393220
  30.2 0.9 %copy-start.21 = (f32[2,128,128]{2,1,0:T(8,128)S(1)}, f32[2,128,128]{2,1,0:T(8,128)}, u32[]{:S(2)}) copy-start(f32[2,128,128]{2,1,0:T(8,128)} %copy-done.20) | copy-start | bytes 393220
  31.1 33.0 %copy-start = (bf16[384,512]{1,0:T(8,128)(2,1)S(1)}, bf16[384,512]{1,0:T(8,128)(2,1)}, u32[]{:S(2)}) copy-start(bf16[384,512]{1,0:T(8,128)(2,1)} %constant.31.clone.table_ref) | copy-start | bytes 1179652

commit v4 on v2

--- a/solution.py
+++ b/solution.py
@@ -134,24 +134,27 @@
 
 
 def spectrum_kernel(
-    mask_hbm, right_hbm, left_hbm, after_hbm, re_ref, im_ref, mask_ref, right_ref, left_ref, sems
+    mask_hbm, right_hbm, left_hbm, after_any, re_ref, im_ref, mask_ref, right_ref, left_ref, sems
 ):
     half_tile = TILE // 2
     pairs = [(right_hbm, right_ref)]
     for t in range(2):
         for part in range(2):
-            rows = pl.ds(part * half_tile, half_tile)
-            pairs.append((mask_hbm.at[t, rows], mask_ref.at[t, rows]))
+            piece = pl.ds(part * half_tile, half_tile)
+            pairs.append((mask_hbm.at[t, piece], mask_ref.at[t, piece]))
     pairs.insert(3, (left_hbm, left_ref))
     loads = [pltpu.make_async_copy(*pair, sems.at[n]) for n, pair in enumerate(pairs)]
-    for load in loads:
+    for load in loads[:3]:
         load.start()
-    loads[0].wait()
     for t in range(2):
         highs = []
         lows = []
         for part in range(2):
             loads[1 + 3 * t + part].wait()
+            if t == 0 and part == 0:
+                loads[0].wait()
+                for load in loads[3:]:
+                    load.start()
             high, low = split(mask_ref[t, part * half_tile : (part + 1) * half_tile])
             high, low = split(
                 mm(high, right_ref[0]) + mm(high, right_ref[1]) + mm(low, right_ref[0])
@@ -247,7 +250,7 @@
     adj_ref[...] = jnp.zeros_like(adj_ref)
     term_ref[...] = jnp.zeros_like(term_ref)
     rows = 2 * ROWS
-    for load in loads[:5]:
+    for load in loads[:6]:
         load.wait()
     pupil_re, pupil_im = [jnp.concatenate([pupil_ref[n], pupil_ref[n]], 1) for n in range(2)]
     pupil_re_odd = jnp.where(first_half, -pupil_re, pupil_re)
@@ -260,7 +263,7 @@
     def window_of(k):
         return place_of(point_ref[k >> 1, 0, k & 1])
 
-    def windows(step, carry):
+    def windows(step):
         for inner in range(8):
             k = step * 8 + inner
             row_pos, col_pos = window_of(k)
@@ -289,12 +292,8 @@
                 0,
             )
             half_ref[pl.ds(pl.multiple_of(k * rows, rows), rows), :] = split_cols(half)
-        return carry
-
-    lax.fori_loop(0, POINTS // 8, windows, 0)
-    loads[5].wait()
-
-    def fields(step, carry):
+
+    def fields(step):
         field = mm(
             half_ref[pl.ds(pl.multiple_of(step * 8 * rows, 8 * rows), 8 * rows), :], col_ref[...]
         )
@@ -307,9 +306,18 @@
                 one[:, :WIDTH] * one[:, :WIDTH] + one[:, WIDTH:] * one[:, WIDTH:]
             )
         total_ref[...] = total
-        return carry
-
-    lax.fori_loop(0, POINTS // 8, fields, 0)
+
+    def in_turn(first, second):
+        def both(step, carry):
+            second(step - 1)
+            first(step)
+            return carry
+
+        first(0)
+        lax.fori_loop(1, POINTS // 8, both, 0)
+        second(POINTS // 8 - 1)
+
+    in_turn(windows, fields)
 
     for load in loads[6:]:
         load.wait()
@@ -327,7 +335,7 @@
         slope_ref[t * ROWS : (t + 1) * ROWS] = (8.0 * live) * slope
     slope_ref[:, :WIDTH] = mm(split_cols(slope_ref[...]), lower_ref[...])
 
-    def columns_back(step, carry):
+    def columns_back(step):
         slope = slope_ref[:, :WIDTH]
         highs = []
         lows = []
@@ -349,11 +357,8 @@
         back_ref[pl.ds(pl.multiple_of(step * 8 * rows, 8 * rows), 8 * rows), :] = (
             half[:, :WIDTH] + half[:, WIDTH:] + rest
         )
-        return carry
-
-    lax.fori_loop(0, POINTS // 8, columns_back, 0)
-
-    def rows_back(step, carry):
+
+    def rows_back(step):
         for inner in range(8):
             k = step * 8 + inner
             row_pos, col_pos = window_of(k)
@@ -373,9 +378,8 @@
                 )
                 adj_ref[t, pl.ds(row_pos, BAND), :] += jnp.where(inside, spread, 0.0)
                 adj_ref[2 + t, pl.ds(row_pos, BAND), :] += jnp.where(inside, 0.0, spread)
-        return carry
-
-    lax.fori_loop(0, POINTS // 8, rows_back, 0)
+
+    in_turn(columns_back, rows_back)
 
     lane = lax.broadcasted_iota(jnp.int32, (WIDTH, WIDTH), 1)
     tops = []
@@ -435,7 +439,9 @@
 ):
     held = {name: jnp.asarray(table) for name, table in constants().items()}
     smem = pl.BlockSpec(memory_space=pltpu.SMEM)
+    free = pl.BlockSpec(memory_space=pl.ANY)
     hbm = pl.BlockSpec(memory_space=pltpu.HBM)
+    roomy = pltpu.CompilerParams(vmem_limit_bytes=56 * 1024 * 1024)
 
     mine = pl.pallas_call(
         pack_kernel,
@@ -445,18 +451,17 @@
     )(source_index, source_weight)
     points = lax.all_to_all(mine, "src", 0, 0)
 
-    roomy = pltpu.CompilerParams(vmem_limit_bytes=56 * 1024 * 1024)
     stored = [mask_field, held["spec_right"], held["spec_left"]]
     spec_shape = jax.ShapeDtypeStruct((2, WIDTH, WIDTH), f32)
     spec_re, spec_im = pl.pallas_call(
         spectrum_kernel,
-        in_specs=[hbm] * 4,
+        in_specs=[hbm] * 3 + [free],
         out_shape=[spec_shape, spec_shape],
         scratch_shapes=[pltpu.VMEM(a.shape, a.dtype) for a in stored]
         + [pltpu.SemaphoreType.DMA((6,))],
         compiler_params=roomy,
         cost_estimate=pl.CostEstimate(
-            flops=1_200_000_000, bytes_accessed=3_000_000, transcendentals=0
+            flops=2_400_000_000, bytes_accessed=3_000_000, transcendentals=0
         ),
         name="spectrum",
     )(*stored, mine)
@@ -471,8 +476,7 @@
         landing[n] = pltpu.VMEM(stored[n].shape[1:], bf16)
     blocks = pl.pallas_call(
         main_kernel,
-        in_specs=[hbm] * len(stored),
-        out_specs=pl.BlockSpec(memory_space=pltpu.VMEM),
+        in_specs=[free] * 4 + [hbm] * (len(stored) - 4),
         out_shape=jax.ShapeDtypeStruct((SRC, CHUNK, WIDTH), f32),
         scratch_shapes=landing
         + [
@@ -487,12 +491,13 @@
         ],
         compiler_params=roomy,
         cost_estimate=pl.CostEstimate(
-            flops=3_000_000_000, bytes_accessed=5_000_000, transcendentals=300_000
+            flops=8_000_000_000, bytes_accessed=5_000_000, transcendentals=300_000
         ),
         name="fields",
     )(*stored)
 
-    chunks = lax.all_to_all(blocks, "src", 0, 0)
+    chunks = lax.all_to_all(blocks.reshape(SRC, 1, CHUNK * WIDTH), "src", 0, 0)
+    chunks = chunks.reshape(SRC, CHUNK, WIDTH)
     grad_mask, term = pl.pallas_call(
         image_kernel,
         out_shape=[

time: 80.3 us -> 78.6 us (0.979)
  Pallas kernels: 18.5 us -> 16.9 us
    pallas_call x2, Pallas kernels: 16.4 us -> 14.7 us  [the longest x1 9.46 us: per_device(): pl.pallas_call(main_kernel, in_specs=[free] * 4 + [hbm] * (len(stored) -...]
where the time goes in v4:
time: 78.6 us; the launch traced here: 78.3 us
  blocking collectives  45.8 us (58%)
  Pallas kernels  16.9 us (22%)
  starting transfers between devices  10.2 us (13%)
  waiting for transfers between devices  3.53 us (4%)
    all_to_all x1, blocking collectives, per_device(): chunks = lax.all_to_all(blocks.reshape(SRC, 1, CHUNK * WIDTH), 'src', 0, 0)  24.3 us
    all_to_all x1, blocking collectives, per_device(): term = lax.all_to_all(term, 'clip', 0, 0)  21.5 us
    all_to_all x1, starting transfers between devices, per_device(): points = lax.all_to_all(mine, 'src', 0, 0)  10.2 us
    pallas_call x1, Pallas kernels, per_device(): pl.pallas_call(main_kernel, in_specs=[free] * 4 + [hbm] * (len(stored) -...  9.46 us
    pallas_call x1, Pallas kernels, per_device(): pl.pallas_call(spectrum_kernel, in_specs=[hbm] * 3 + [free], out_shape=[s...  5.27 us
    all_to_all x1, waiting for transfers between devices, per_device(): points = lax.all_to_all(mine, 'src', 0, 0)  3.53 us
  transfers between devices with their start and end apart: 1, of which 1 were waited for; matrix products, arithmetic and copies ran while one was open for 0% of the time, Pallas kernels for 7%

profile of v4, /device:TPU:1, one launch (start us, length us, event | category | flops | bytes accessed | tf_op | source)
XLA Modules:
  0.0 78.3 jit_solution(5380696914374627863)
XLA Ops:
  0.6 1.3 %pack.1.after_any = f32[16,1,128]{2,1,0:T(1,128)} custom-call(s32[2]{0:T(128)} %index_ref.1, f32[2]{0:T(128)} %weight_ref.1), custom_call_target="tpu_custom_call" | custom-call | tf_op jit(solution)/shard_map/pack/pallas_call | solution.py:446
  1.9 10.2 %all-to-all-start = ((f32[16,1,128]{2,1,0:T(1,128)}), f32[16,1,128]{2,1,0:T(1,128)S(1)}, u32[]{:S(2)}, u32[]{:S(2)}) async-start(f32[16,1,128]{2,1,0:T(1,128)} %pack.1.after_any), calls=%async_computation | async-start | bytes 16384 | tf_op jit(solution)/shard_map/all_to_all | solution.py:452
  12.1 5.3 %spectrum.1 = (f32[2,128,128]{2,1,0:T(8,128)}, f32[2,128,128]{2,1,0:T(8,128)}) custom-call(f32[2,512,512]{2,1,0:T(8,128)} %mask_hbm.1, bf16[2,512,256]{2,1,0:T(8,128)(2,1)} %constant.22.clone.right_hbm.lines_hbm, bf16[2,256,512]{2,1,0:T(8,128)(2,1)} %constant.23.clone.left_hbm, f32[16,1,128]{2,1,0:T(1,128)} %pack.1.after_any), custom_call_target="tpu_custom_call" | custom-call | flops 2400000000 | bytes 3000000 | tf_op jit(solution)/shard_map/spectrum/pallas_call | solution.py:456
  17.4 3.5 %all-to-all-done.point_hbm = f32[16,1,128]{2,1,0:T(1,128)S(1)} async-done(((f32[16,1,128]{2,1,0:T(1,128)}), f32[16,1,128]{2,1,0:T(1,128)S(1)}, u32[]{:S(2)}, u32[]{:S(2)}) %all-to-all-start) | async-done | bytes 8224 | tf_op jit(solution)/shard_map/all_to_all | solution.py:452
  20.9 0.0 copy-start.1
  20.9 0.6 copy-done.1
  21.5 0.0 copy-start
  21.5 9.5 %fields.1 = f32[16,72,128]{2,1,0:T(8,128)} custom-call(f32[16,1,128]{2,1,0:T(1,128)} %copy-done.1, s32[16]{0:T(128)} %count_hbm.1, f32[2,128,128]{2,1,0:T(8,128)} %get-tuple-element.6.re_hbm, f32[2,128,128]{2,1,0:T(8,128)} %get-tuple-element.7.im_hbm, f32[2,64,64]{2,1,0:T(8,128)} %pupil_hbm.1, bf16[16,128,128]{2,1,0:T(8,128)(2,1)} %constant.24.clone.row_hbm, ...), custom_call_target="tpu_custom_call" | custom-call | flops 8000000000 | bytes 5000000 | tf_op jit(solution)/shard_map/fields/pallas_call | solution.py:477
  31.0 24.3 %all_to_all.15 = f32[16,1,9216]{2,1,0:T(1,128)S(1)} all-to-all(f32[16,1,9216]{2,1,0:T(1,128)} %bitcast.3), channel_id=1, replica_groups=mesh['clip'=32,'src'=16] {'src'}, dimensions={0} | all-to-all | bytes 1179648 | tf_op jit(solution)/shard_map/all_to_all | solution.py:499
  55.3 0.0 copy-done
  55.3 0.9 %image.1 = (f32[2,32,512]{2,1,0:T(8,128)}, f32[32,8,128]{2,1,0:T(8,128)S(1)}) custom-call(f32[16,72,128]{2,1,0:T(8,128)S(1)} %bitcast.2, bf16[384,512]{1,0:T(8,128)(2,1)S(1)} %copy-done), custom_call_target="tpu_custom_call" | custom-call | flops 100000000 | bytes 1000000 | tf_op jit(solution)/shard_map/image/pallas_call | solution.py:501
  56.1 21.5 %all_to_all.16 = f32[32,8,128]{2,1,0:T(8,128)S(1)} all-to-all(f32[32,8,128]{2,1,0:T(8,128)S(1)} %get-tuple-element.9), channel_id=1, replica_groups=mesh['clip'=32,'src'=16] {'clip'}, dimensions={0} | all-to-all | bytes 262144 | tf_op jit(solution)/shard_map/all_to_all | solution.py:513
  77.6 0.7 slice_reduce_fusion
Async XLA Ops:
  1.9 19.0 %all-to-all-start = ((f32[16,1,128]{2,1,0:T(1,128)}), f32[16,1,128]{2,1,0:T(1,128)S(1)}, u32[]{:S(2)}, u32[]{:S(2)}) async-start(f32[16,1,128]{2,1,0:T(1,128)} %pack.1.after_any), calls=%async_computation | async-start | bytes 16384 | tf_op jit(solution)/shard_map/all_to_all | solution.py:452
  20.9 0.6 copy-start.1
  21.5 33.8 %copy-start = (bf16[384,512]{1,0:T(8,128)(2,1)S(1)}, bf16[384,512]{1,0:T(8,128)(2,1)}, u32[]{:S(2)}) copy-start(bf16[384,512]{1,0:T(8,128)(2,1)} %constant.31.clone.table_ref) | copy-start | bytes 1179652

commit v5 on v4

--- a/solution.py
+++ b/solution.py
@@ -193,6 +193,7 @@
     row_back_hbm,
     fold_hbm,
     lines_hbm,
+    out_any,
     out_ref,
     point_ref,
     count_ref,
@@ -404,6 +405,7 @@
             0,
         )
     )
+    stores = []
     for block in range(4):
         at_rows = slice(block * WIDTH, (block + 1) * WIDTH)
         table_high = right_ref[0, at_rows, :]
@@ -415,6 +417,21 @@
             out_ref[owner, :ROWS, :] = own_rows[:, :WIDTH]
             out_ref[owner, ROWS:rows, :] = own_rows[:, WIDTH : 2 * WIDTH]
             out_ref[owner, rows:, :] = flat[:8] + term_ref[owner]
+        owners = pl.ds(block * 4, 4)
+        stores.append(
+            pltpu.make_async_copy(
+                out_ref.at[owners], out_any.at[owners], sems.at[len(loads) + block]
+            )
+        )
+        stores[-1].start()
+    for store in stores:
+        store.wait()
+
+
+def table_kernel(after_any, table_any, out_ref, sem):
+    load = pltpu.make_async_copy(table_any, out_ref, sem)
+    load.start()
+    load.wait()
 
 
 def image_kernel(chunk_ref, table_ref, out_ref, term_ref):
@@ -431,7 +448,9 @@
         column = jnp.sum(jnp.where(diagonal, flat[t : t + 1], 0.0), 1, keepdims=True)
         out_ref[t] = image[t * ROWS : (t + 1) * ROWS] + column * (1.0 / math.sqrt(TILE))
     sums = jnp.sum(last, 1, keepdims=True) * (1.0 / (TILE * TILE))
-    term_ref[...] = jnp.broadcast_to(jnp.broadcast_to(sums, (8, WIDTH))[None], term_ref.shape)
+    lane = lax.broadcasted_iota(jnp.int32, (1, WIDTH), 1)
+    terms = jnp.where(lane == 0, sums[2:3], jnp.where(lane == 1, sums[3:4], 0.0))
+    term_ref[...] = jnp.broadcast_to(terms[None], term_ref.shape)
 
 
 def per_device(
@@ -477,8 +496,10 @@
     blocks = pl.pallas_call(
         main_kernel,
         in_specs=[free] * 4 + [hbm] * (len(stored) - 4),
+        out_specs=free,
         out_shape=jax.ShapeDtypeStruct((SRC, CHUNK, WIDTH), f32),
-        scratch_shapes=landing
+        scratch_shapes=[pltpu.VMEM((SRC, CHUNK, WIDTH), f32)]
+        + landing
         + [
             pltpu.VMEM((POINTS * 2 * ROWS, 3 * WIDTH), bf16),
             pltpu.VMEM((POINTS, 2 * ROWS, 2 * WIDTH), f32),
@@ -487,7 +508,7 @@
             pltpu.VMEM((POINTS * 2 * ROWS, WIDTH), f32),
             pltpu.VMEM((4, WIDTH, WIDTH), f32),
             pltpu.VMEM((SRC, 8, WIDTH), f32),
-            pltpu.SemaphoreType.DMA((len(stored),)),
+            pltpu.SemaphoreType.DMA((len(stored) + 4,)),
         ],
         compiler_params=roomy,
         cost_estimate=pl.CostEstimate(
@@ -498,20 +519,30 @@
 
     chunks = lax.all_to_all(blocks.reshape(SRC, 1, CHUNK * WIDTH), "src", 0, 0)
     chunks = chunks.reshape(SRC, CHUNK, WIDTH)
+    small = pltpu.CompilerParams(vmem_limit_bytes=12 * 1024 * 1024)
+    table = pl.pallas_call(
+        table_kernel,
+        in_specs=[free, free],
+        out_shape=jax.ShapeDtypeStruct(held["image"].shape, bf16),
+        scratch_shapes=[pltpu.SemaphoreType.DMA],
+        compiler_params=small,
+        cost_estimate=pl.CostEstimate(flops=0, bytes_accessed=800_000, transcendentals=0),
+        name="table",
+    )(blocks, held["image"])
     grad_mask, term = pl.pallas_call(
         image_kernel,
         out_shape=[
             jax.ShapeDtypeStruct((2, ROWS, TILE), f32),
-            jax.ShapeDtypeStruct((clips, 8, WIDTH), f32),
+            jax.ShapeDtypeStruct((clips, 1, WIDTH), f32),
         ],
-        compiler_params=pltpu.CompilerParams(vmem_limit_bytes=12 * 1024 * 1024),
+        compiler_params=small,
         cost_estimate=pl.CostEstimate(
             flops=100_000_000, bytes_accessed=1_000_000, transcendentals=0
         ),
         name="image",
-    )(chunks, held["image"])
+    )(chunks, table)
     term = lax.all_to_all(term, "clip", 0, 0)
-    grad_source = jnp.sum(term[:, 2:4, 0], 0)
+    grad_source = jnp.sum(term[:, 0, :2], 0)
     return (grad_mask, grad_source)
 
 

time: 78.6 us -> 77.4 us (0.985)
  blocking collectives: 45.8 us -> 20.8 us
  waiting for transfers between devices: 3.53 us -> 20.6 us
  starting transfers between devices: 10.2 us -> 15.8 us
  local copies, waits for them, and re-layouts: 0.59 us -> 1.68 us
    all_to_all x1 -> x0, blocking collectives: 24.3 us -> none  [per_device(): chunks = lax.all_to_all(blocks.reshape(SRC, 1, CHUNK * WIDTH), 'src', 0, 0)]
    all_to_all x0 -> x1, waiting for transfers between devices: none -> 17.1 us  [per_device(): chunks = lax.all_to_all(blocks.reshape(SRC, 1, CHUNK * WIDTH), 'src', 0, 0)]
    all_to_all x0 -> x1, starting transfers between devices: none -> 5.55 us  [per_device(): chunks = lax.all_to_all(blocks.reshape(SRC, 1, CHUNK * WIDTH), 'src', 0, 0)]
    unnamed x4 -> x6, local copies, waits for them, and re-layouts: 0.59 us -> 1.68 us
  transfers between devices with their start and end apart: 1 -> 2, of which waited for: 1 -> 2; matrix products, arithmetic and copies ran while one was open for 0% -> 0% of each run, Pallas kernels for 7% -> 7%
where the time goes in v5:
time: 77.4 us; the launch traced here: 77 us
  blocking collectives  20.8 us (27%)
  waiting for transfers between devices  20.6 us (27%)
  Pallas kernels  16.9 us (22%)
  starting transfers between devices  15.8 us (20%)
  local copies, waits for them, and re-layouts  1.68 us (2%)
    all_to_all x1, blocking collectives, per_device(): term = lax.all_to_all(term, 'clip', 0, 0)  20.8 us
    all_to_all x1, waiting for transfers between devices, per_device(): chunks = lax.all_to_all(blocks.reshape(SRC, 1, CHUNK * WIDTH), 'src', 0, 0)  17.1 us
    all_to_all x1, starting transfers between devices, per_device(): points = lax.all_to_all(mine, 'src', 0, 0)  10.2 us
    pallas_call x1, Pallas kernels, per_device(): pl.pallas_call(main_kernel, in_specs=[free] * 4 + [hbm] * (len(stored) -...  9.33 us
    all_to_all x1, starting transfers between devices, per_device(): chunks = lax.all_to_all(blocks.reshape(SRC, 1, CHUNK * WIDTH), 'src', 0, 0)  5.55 us
    pallas_call x1, Pallas kernels, per_device(): pl.pallas_call(spectrum_kernel, in_specs=[hbm] * 3 + [free], out_shape=[s...  5.28 us
    all_to_all x1, waiting for transfers between devices, per_device(): points = lax.all_to_all(mine, 'src', 0, 0)  3.53 us
    unnamed x6, local copies, waits for them, and re-layouts  1.68 us
  transfers between devices with their start and end apart: 2, of which 2 were waited for; matrix products, arithmetic and copies ran while one was open for 0% of the time, Pallas kernels for 7%

profile of v5, /device:TPU:1, one launch (start us, length us, event | category | flops | bytes accessed | tf_op | source)
XLA Modules:
  0.0 77.0 jit_solution(334093870740245613)
XLA Ops:
  0.6 1.3 %pack.1.after_any = f32[16,1,128]{2,1,0:T(1,128)} custom-call(s32[2]{0:T(128)} %index_ref.1, f32[2]{0:T(128)} %weight_ref.1), custom_call_target="tpu_custom_call" | custom-call | tf_op jit(solution)/shard_map/pack/pallas_call | solution.py:465
  1.9 10.2 %all-to-all-start = ((f32[16,1,128]{2,1,0:T(1,128)}), f32[16,1,128]{2,1,0:T(1,128)S(1)}, u32[]{:S(2)}, u32[]{:S(2)}) async-start(f32[16,1,128]{2,1,0:T(1,128)} %pack.1.after_any), calls=%async_computation | async-start | bytes 16384 | tf_op jit(solution)/shard_map/all_to_all | solution.py:471
  12.1 5.3 %spectrum.1 = (f32[2,128,128]{2,1,0:T(8,128)}, f32[2,128,128]{2,1,0:T(8,128)}) custom-call(f32[2,512,512]{2,1,0:T(8,128)} %mask_hbm.1, bf16[2,512,256]{2,1,0:T(8,128)(2,1)} %constant.22.clone.right_hbm.lines_hbm, bf16[2,256,512]{2,1,0:T(8,128)(2,1)} %constant.23.clone.left_hbm, f32[16,1,128]{2,1,0:T(1,128)} %pack.1.after_any), custom_call_target="tpu_custom_call" | custom-call | flops 2400000000 | bytes 3000000 | tf_op jit(solution)/shard_map/spectrum/pallas_call | solution.py:475
  17.4 3.5 %all-to-all-done.point_hbm = f32[16,1,128]{2,1,0:T(1,128)S(1)} async-done(((f32[16,1,128]{2,1,0:T(1,128)}), f32[16,1,128]{2,1,0:T(1,128)S(1)}, u32[]{:S(2)}, u32[]{:S(2)}) %all-to-all-start) | async-done | bytes 8224 | tf_op jit(solution)/shard_map/all_to_all | solution.py:471
  21.0 0.0 copy-start.2
  21.0 0.6 copy-done.2
  21.5 0.0 copy-start.1
  21.5 9.3 %fields.1.after_any = f32[16,72,128]{2,1,0:T(8,128)} custom-call(f32[16,1,128]{2,1,0:T(1,128)} %copy-done.2, s32[16]{0:T(128)} %count_hbm.1, f32[2,128,128]{2,1,0:T(8,128)} %get-tuple-element.6.re_hbm, f32[2,128,128]{2,1,0:T(8,128)} %get-tuple-element.7.im_hbm, f32[2,64,64]{2,1,0:T(8,128)} %pupil_hbm.1, bf16[16,128,128]{2,1,0:T(8,128)(2,1)} %constant.24.clone.row_hbm, ...), custom_call_target="tpu_custom_call" | custom-call | flops 8000000000 | bytes 5000000 | tf_op jit(solution)/shard_map/fields/pallas_call | solution.py:496
  30.9 5.5 %all-to-all-start.1 = ((f32[16,1,9216]{2,1,0:T(1,128)}), f32[16,1,9216]{2,1,0:T(1,128)S(1)}, u32[]{:S(2)}, u32[]{:S(2)}) async-start(f32[16,1,9216]{2,1,0:T(1,128)} %bitcast.3), calls=%async_computation.1 | async-start | bytes 1179648 | tf_op jit(solution)/shard_map/all_to_all | solution.py:520
  36.4 0.0 copy-done.1
  36.5 0.0 copy-start
  36.5 1.1 %copy-done = f32[16,72,128]{2,1,0:T(8,128)S(1)} copy-done((f32[16,72,128]{2,1,0:T(8,128)S(1)}, f32[16,72,128]{2,1,0:T(8,128)}, u32[]{:S(2)}) %copy-start) | copy-done | bytes 589848
  37.5 0.2 table.1.table_ref
  37.7 17.1 %all-to-all-done.1 = f32[16,1,9216]{2,1,0:T(1,128)S(1)} async-done(((f32[16,1,9216]{2,1,0:T(1,128)}), f32[16,1,9216]{2,1,0:T(1,128)S(1)}, u32[]{:S(2)}, u32[]{:S(2)}) %all-to-all-start.1) | async-done | bytes 589856 | tf_op jit(solution)/shard_map/all_to_all | solution.py:520
  54.8 0.9 %image.1 = (f32[2,32,512]{2,1,0:T(8,128)}, f32[32,1,128]{2,1,0:T(1,128)S(1)}) custom-call(f32[16,72,128]{2,1,0:T(8,128)S(1)} %bitcast.2, bf16[384,512]{1,0:T(8,128)(2,1)S(1)} %table.1.table_ref), custom_call_target="tpu_custom_call" | custom-call | flops 100000000 | bytes 1000000 | tf_op jit(solution)/shard_map/image/pallas_call | solution.py:532
  55.7 20.8 %all_to_all.15 = f32[32,1,128]{2,1,0:T(1,128)S(1)} all-to-all(f32[32,1,128]{2,1,0:T(1,128)S(1)} %get-tuple-element.9), channel_id=1, replica_groups=mesh['clip'=32,'src'=16] {'clip'}, dimensions={0} | all-to-all | bytes 32768 | tf_op jit(solution)/shard_map/all_to_all | solution.py:544
  76.5 0.6 slice_reduce_fusion
Async XLA Ops:
  1.9 19.0 %all-to-all-start = ((f32[16,1,128]{2,1,0:T(1,128)}), f32[16,1,128]{2,1,0:T(1,128)S(1)}, u32[]{:S(2)}, u32[]{:S(2)}) async-start(f32[16,1,128]{2,1,0:T(1,128)} %pack.1.after_any), calls=%async_computation | async-start | bytes 16384 | tf_op jit(solution)/shard_map/all_to_all | solution.py:471
  21.0 0.6 copy-start.2
  21.5 14.9 %copy-start.1 = (bf16[384,512]{1,0:T(8,128)(2,1)S(1)}, bf16[384,512]{1,0:T(8,128)(2,1)}, u32[]{:S(2)}) copy-start(bf16[384,512]{1,0:T(8,128)(2,1)} %constant.31.clone.table_any) | copy-start | bytes 1179652
  30.9 23.9 %all-to-all-start.1 = ((f32[16,1,9216]{2,1,0:T(1,128)}), f32[16,1,9216]{2,1,0:T(1,128)S(1)}, u32[]{:S(2)}, u32[]{:S(2)}) async-start(f32[16,1,9216]{2,1,0:T(1,128)} %bitcast.3), calls=%async_computation.1 | async-start | bytes 1179648 | tf_op jit(solution)/shard_map/all_to_all | solution.py:520
  36.5 1.1 %copy-start = (f32[16,72,128]{2,1,0:T(8,128)S(1)}, f32[16,72,128]{2,1,0:T(8,128)}, u32[]{:S(2)}) copy-start(f32[16,72,128]{2,1,0:T(8,128)} %fields.1.after_any) | copy-start | bytes 1769476

commit v6 on v5

--- a/solution.py
+++ b/solution.py
@@ -17,7 +17,7 @@
 ROWS = TILE // SRC
 DOSES = 8
 POINTS = 32
-CHUNK = 2 * ROWS + 8
+CHUNK = 2 * ROWS + 1
 
 f32 = jnp.float32
 bf16 = jnp.bfloat16
@@ -134,28 +134,38 @@
 
 
 def spectrum_kernel(
-    mask_hbm, right_hbm, left_hbm, after_any, re_ref, im_ref, mask_ref, right_ref, left_ref, sems
+    mask_hbm,
+    right_hbm,
+    left_hbm,
+    after_any,
+    re_any,
+    im_any,
+    mask_ref,
+    right_ref,
+    left_ref,
+    re_ref,
+    im_ref,
+    sems,
 ):
-    half_tile = TILE // 2
-    pairs = [(right_hbm, right_ref)]
-    for t in range(2):
-        for part in range(2):
-            piece = pl.ds(part * half_tile, half_tile)
-            pairs.append((mask_hbm.at[t, piece], mask_ref.at[t, piece]))
-    pairs.insert(3, (left_hbm, left_ref))
+    pieces = [(0, 0, 256), (0, 256, 256), (1, 0, 256), (1, 256, 128), (1, 384, 128)]
+    pairs = [
+        (mask_hbm.at[t, pl.ds(at, size)], mask_ref.at[t, pl.ds(at, size)])
+        for t, at, size in pieces
+    ]
+    pairs += [(right_hbm, right_ref), (left_hbm, left_ref)]
     loads = [pltpu.make_async_copy(*pair, sems.at[n]) for n, pair in enumerate(pairs)]
-    for load in loads[:3]:
-        load.start()
+    for n in (5, 0, 1, 6, 2, 3, 4):
+        loads[n].start()
+    loads[5].wait()
+    stores = []
     for t in range(2):
         highs = []
         lows = []
-        for part in range(2):
-            loads[1 + 3 * t + part].wait()
-            if t == 0 and part == 0:
-                loads[0].wait()
-                for load in loads[3:]:
-                    load.start()
-            high, low = split(mask_ref[t, part * half_tile : (part + 1) * half_tile])
+        for n, (tile, at, size) in enumerate(pieces):
+            if tile != t:
+                continue
+            loads[n].wait()
+            high, low = split(mask_ref[t, at : at + size])
             high, low = split(
                 mm(high, right_ref[0]) + mm(high, right_ref[1]) + mm(low, right_ref[0])
             )
@@ -164,10 +174,17 @@
         high = jnp.concatenate(highs, 0)
         low = jnp.concatenate(lows, 0)
         if t == 0:
-            loads[3].wait()
+            loads[6].wait()
         blocks = mm(left_ref[0], high) + mm(left_ref[0], low) + mm(left_ref[1], high)
         re_ref[t] = blocks[:WIDTH, :WIDTH] - blocks[WIDTH:, WIDTH:]
         im_ref[t] = pltpu.roll(-(blocks[WIDTH:, :WIDTH] + blocks[:WIDTH, WIDTH:]), BAND, 1)
+        for n, (source, target) in enumerate(((re_ref, re_any), (im_ref, im_any))):
+            stores.append(
+                pltpu.make_async_copy(source.at[t], target.at[t], sems.at[7 + 2 * t + n])
+            )
+            stores[-1].start()
+    for store in stores:
+        store.wait()
 
 
 def place_of(number):
@@ -406,6 +423,7 @@
         )
     )
     stores = []
+    place = lane[:1]
     for block in range(4):
         at_rows = slice(block * WIDTH, (block + 1) * WIDTH)
         table_high = right_ref[0, at_rows, :]
@@ -413,17 +431,24 @@
         flat = lines[:, 2 * WIDTH :].T
         for n in range(4):
             owner = block * 4 + n
+            base = owner * CHUNK
             own_rows = lines[n * ROWS : (n + 1) * ROWS]
-            out_ref[owner, :ROWS, :] = own_rows[:, :WIDTH]
-            out_ref[owner, ROWS:rows, :] = own_rows[:, WIDTH : 2 * WIDTH]
-            out_ref[owner, rows:, :] = flat[:8] + term_ref[owner]
-        owners = pl.ds(block * 4, 4)
-        stores.append(
-            pltpu.make_async_copy(
-                out_ref.at[owners], out_any.at[owners], sems.at[len(loads) + block]
-            )
-        )
-        stores[-1].start()
+            out_ref[base : base + ROWS, :] = own_rows[:, :WIDTH]
+            out_ref[base + ROWS : base + rows, :] = own_rows[:, WIDTH : 2 * WIDTH]
+            sums = jnp.sum(term_ref[owner], 1, keepdims=True)
+            line = jnp.where(place == rows, sums[2:3], jnp.where(place == rows + 1, sums[3:4], 0.0))
+            for t in (1, 0):
+                turned = pltpu.roll(flat[t : t + 1], (WIDTH + (t - n) * ROWS) % WIDTH, 1)
+                line = jnp.where(place < (t + 1) * ROWS, turned, line)
+            out_ref[base + rows : base + CHUNK, :] = line
+        if block % 2:
+            owners = pl.ds((block - 1) * 4 * CHUNK, 8 * CHUNK)
+            stores.append(
+                pltpu.make_async_copy(
+                    out_ref.at[owners], out_any.at[owners], sems.at[len(loads) + block // 2]
+                )
+            )
+            stores[-1].start()
     for store in stores:
         store.wait()
 
@@ -435,21 +460,19 @@
 
 
 def image_kernel(chunk_ref, table_ref, out_ref, term_ref):
-    me = lax.axis_index("src")
     rows = 2 * ROWS
-    total = jnp.sum(chunk_ref[...], 0)
-    image = mm(split_cols(total[:rows]), table_ref[...])
-    last = total[rows:]
-    flat = pltpu.roll(last, (WIDTH - (me & 3) * ROWS) & (WIDTH - 1), 1)
-    diagonal = lax.broadcasted_iota(jnp.int32, (ROWS, WIDTH), 0) == lax.broadcasted_iota(
-        jnp.int32, (ROWS, WIDTH), 1
-    )
+    total = chunk_ref[:rows]
+    last = chunk_ref[rows:CHUNK]
+    for n in range(1, SRC):
+        total += chunk_ref[n * CHUNK : n * CHUNK + rows]
+        last += chunk_ref[n * CHUNK + rows : (n + 1) * CHUNK]
+    image = mm(split_cols(total), table_ref[...])
+    row = lax.broadcasted_iota(jnp.int32, (ROWS, WIDTH), 0)
+    lane = lax.broadcasted_iota(jnp.int32, (ROWS, WIDTH), 1)
     for t in range(2):
-        column = jnp.sum(jnp.where(diagonal, flat[t : t + 1], 0.0), 1, keepdims=True)
+        column = jnp.sum(jnp.where(lane == row + t * ROWS, last, 0.0), 1, keepdims=True)
         out_ref[t] = image[t * ROWS : (t + 1) * ROWS] + column * (1.0 / math.sqrt(TILE))
-    sums = jnp.sum(last, 1, keepdims=True) * (1.0 / (TILE * TILE))
-    lane = lax.broadcasted_iota(jnp.int32, (1, WIDTH), 1)
-    terms = jnp.where(lane == 0, sums[2:3], jnp.where(lane == 1, sums[3:4], 0.0))
+    terms = jnp.where(lane[:1] < 2, pltpu.roll(last, WIDTH - rows, 1), 0.0) * (1.0 / (TILE * TILE))
     term_ref[...] = jnp.broadcast_to(terms[None], term_ref.shape)
 
 
@@ -475,9 +498,11 @@
     spec_re, spec_im = pl.pallas_call(
         spectrum_kernel,
         in_specs=[hbm] * 3 + [free],
+        out_specs=[free, free],
         out_shape=[spec_shape, spec_shape],
         scratch_shapes=[pltpu.VMEM(a.shape, a.dtype) for a in stored]
-        + [pltpu.SemaphoreType.DMA((6,))],
+        + [pltpu.VMEM(spec_shape.shape, f32)] * 2
+        + [pltpu.SemaphoreType.DMA((11,))],
         compiler_params=roomy,
         cost_estimate=pl.CostEstimate(
             flops=2_400_000_000, bytes_accessed=3_000_000, transcendentals=0
@@ -497,8 +522,8 @@
         main_kernel,
         in_specs=[free] * 4 + [hbm] * (len(stored) - 4),
         out_specs=free,
-        out_shape=jax.ShapeDtypeStruct((SRC, CHUNK, WIDTH), f32),
-        scratch_shapes=[pltpu.VMEM((SRC, CHUNK, WIDTH), f32)]
+        out_shape=jax.ShapeDtypeStruct((SRC * CHUNK, WIDTH), f32),
+        scratch_shapes=[pltpu.VMEM((SRC * CHUNK, WIDTH), f32)]
         + landing
         + [
             pltpu.VMEM((POINTS * 2 * ROWS, 3 * WIDTH), bf16),
@@ -518,7 +543,7 @@
     )(*stored)
 
     chunks = lax.all_to_all(blocks.reshape(SRC, 1, CHUNK * WIDTH), "src", 0, 0)
-    chunks = chunks.reshape(SRC, CHUNK, WIDTH)
+    chunks = chunks.reshape(SRC * CHUNK, WIDTH)
     small = pltpu.CompilerParams(vmem_limit_bytes=12 * 1024 * 1024)
     table = pl.pallas_call(
         table_kernel,

time: 77.4 us -> 76.2 us (0.984)
  waiting for transfers between devices: 20.6 us -> 19.7 us
    all_to_all x1, waiting for transfers between devices: 17.1 us -> 16.1 us  [per_device(): chunks = lax.all_to_all(blocks.reshape(SRC, 1, CHUNK * WIDTH), 'src', 0, 0)]
where the time goes in v6:
time: 76.2 us; the launch traced here: 75.9 us
  blocking collectives  20.5 us (27%)
  waiting for transfers between devices  19.7 us (26%)
  Pallas kernels  17 us (22%)
  starting transfers between devices  15.8 us (21%)
  local copies, waits for them, and re-layouts  1.66 us (2%)
    all_to_all x1, blocking collectives, per_device(): term = lax.all_to_all(term, 'clip', 0, 0)  20.5 us
    all_to_all x1, waiting for transfers between devices, per_device(): chunks = lax.all_to_all(blocks.reshape(SRC, 1, CHUNK * WIDTH), 'src', 0, 0)  16.1 us
    all_to_all x1, starting transfers between devices, per_device(): points = lax.all_to_all(mine, 'src', 0, 0)  10.2 us
    pallas_call x1, Pallas kernels, per_device(): pl.pallas_call(main_kernel, in_specs=[free] * 4 + [hbm] * (len(stored) -...  9.45 us
    all_to_all x1, starting transfers between devices, per_device(): chunks = lax.all_to_all(blocks.reshape(SRC, 1, CHUNK * WIDTH), 'src', 0, 0)  5.55 us
    pallas_call x1, Pallas kernels, per_device(): pl.pallas_call(spectrum_kernel, in_specs=[hbm] * 3 + [free], out_specs=[f...  5.27 us
    all_to_all x1, waiting for transfers between devices, per_device(): points = lax.all_to_all(mine, 'src', 0, 0)  3.53 us
    unnamed x6, local copies, waits for them, and re-layouts  1.66 us
  transfers between devices with their start and end apart: 2, of which 2 were waited for; matrix products, arithmetic and copies ran while one was open for 0% of the time, Pallas kernels for 7%

profile of v6, /device:TPU:1, one launch (start us, length us, event | category | flops | bytes accessed | tf_op | source)
XLA Modules:
  0.0 75.9 jit_solution(15102669895245777201)
XLA Ops:
  0.6 1.3 %pack.1.after_any = f32[16,1,128]{2,1,0:T(1,128)} custom-call(s32[2]{0:T(128)} %index_ref.1, f32[2]{0:T(128)} %weight_ref.1), custom_call_target="tpu_custom_call" | custom-call | tf_op jit(solution)/shard_map/pack/pallas_call | solution.py:488
  1.9 10.2 %all-to-all-start = ((f32[16,1,128]{2,1,0:T(1,128)}), f32[16,1,128]{2,1,0:T(1,128)S(1)}, u32[]{:S(2)}, u32[]{:S(2)}) async-start(f32[16,1,128]{2,1,0:T(1,128)} %pack.1.after_any), calls=%async_computation | async-start | bytes 16384 | tf_op jit(solution)/shard_map/all_to_all | solution.py:494
  12.1 5.3 %spectrum.1 = (f32[2,128,128]{2,1,0:T(8,128)}, f32[2,128,128]{2,1,0:T(8,128)}) custom-call(f32[2,512,512]{2,1,0:T(8,128)} %mask_hbm.1, bf16[2,512,256]{2,1,0:T(8,128)(2,1)} %constant.22.clone.right_hbm.lines_hbm, bf16[2,256,512]{2,1,0:T(8,128)(2,1)} %constant.23.clone.left_hbm, f32[16,1,128]{2,1,0:T(1,128)} %pack.1.after_any), custom_call_target="tpu_custom_call" | custom-call | flops 2400000000 | bytes 3000000 | tf_op jit(solution)/shard_map/spectrum/pallas_call | solution.py:498
  17.4 3.5 %all-to-all-done.point_hbm = f32[16,1,128]{2,1,0:T(1,128)S(1)} async-done(((f32[16,1,128]{2,1,0:T(1,128)}), f32[16,1,128]{2,1,0:T(1,128)S(1)}, u32[]{:S(2)}, u32[]{:S(2)}) %all-to-all-start) | async-done | bytes 8224 | tf_op jit(solution)/shard_map/all_to_all | solution.py:494
  21.0 0.0 copy-start.2
  21.0 0.6 copy-done.2
  21.5 0.0 copy-start.1
  21.5 9.4 %fields.1.after_any = f32[1040,128]{1,0:T(8,128)} custom-call(f32[16,1,128]{2,1,0:T(1,128)} %copy-done.2, s32[16]{0:T(128)} %count_hbm.1, f32[2,128,128]{2,1,0:T(8,128)} %get-tuple-element.6.re_hbm, f32[2,128,128]{2,1,0:T(8,128)} %get-tuple-element.7.im_hbm, f32[2,64,64]{2,1,0:T(8,128)} %pupil_hbm.1, bf16[16,128,128]{2,1,0:T(8,128)(2,1)} %constant.24.clone.row_hbm, ...), custom_call_target="tpu_custom_call" | custom-call | flops 8000000000 | bytes 5000000 | tf_op jit(solution)/shard_map/fields/pallas_call | solution.py:521
  31.0 5.5 %all-to-all-start.1 = ((f32[16,1,8320]{2,1,0:T(1,128)}), f32[16,1,8320]{2,1,0:T(1,128)S(1)}, u32[]{:S(2)}, u32[]{:S(2)}) async-start(f32[16,1,8320]{2,1,0:T(1,128)} %bitcast.2), calls=%async_computation.1 | async-start | bytes 1064960 | tf_op jit(solution)/shard_map/all_to_all | solution.py:545
  36.6 0.0 copy-done.1
  36.6 0.0 copy-start
  36.6 1.1 %copy-done = f32[1040,128]{1,0:T(8,128)S(1)} copy-done((f32[1040,128]{1,0:T(8,128)S(1)}, f32[1040,128]{1,0:T(8,128)}, u32[]{:S(2)}) %copy-start) | copy-done | bytes 532504
  37.6 0.2 table.1.table_ref
  37.8 16.1 %all-to-all-done.1 = f32[16,1,8320]{2,1,0:T(1,128)S(1)} async-done(((f32[16,1,8320]{2,1,0:T(1,128)}), f32[16,1,8320]{2,1,0:T(1,128)S(1)}, u32[]{:S(2)}, u32[]{:S(2)}) %all-to-all-start.1) | async-done | bytes 532512 | tf_op jit(solution)/shard_map/all_to_all | solution.py:545
  54.0 0.9 %image.1 = (f32[2,32,512]{2,1,0:T(8,128)}, f32[32,1,128]{2,1,0:T(1,128)S(1)}) custom-call(f32[1040,128]{1,0:T(8,128)S(1)} %bitcast.3, bf16[384,512]{1,0:T(8,128)(2,1)S(1)} %table.1.table_ref), custom_call_target="tpu_custom_call" | custom-call | flops 100000000 | bytes 1000000 | tf_op jit(solution)/shard_map/image/pallas_call | solution.py:557
  54.8 20.5 %all_to_all.15 = f32[32,1,128]{2,1,0:T(1,128)S(1)} all-to-all(f32[32,1,128]{2,1,0:T(1,128)S(1)} %get-tuple-element.9), channel_id=1, replica_groups=mesh['clip'=32,'src'=16] {'clip'}, dimensions={0} | all-to-all | bytes 32768 | tf_op jit(solution)/shard_map/all_to_all | solution.py:569
  75.3 0.6 slice_reduce_fusion
Async XLA Ops:
  1.9 19.0 %all-to-all-start = ((f32[16,1,128]{2,1,0:T(1,128)}), f32[16,1,128]{2,1,0:T(1,128)S(1)}, u32[]{:S(2)}, u32[]{:S(2)}) async-start(f32[16,1,128]{2,1,0:T(1,128)} %pack.1.after_any), calls=%async_computation | async-start | bytes 16384 | tf_op jit(solution)/shard_map/all_to_all | solution.py:494
  21.0 0.6 copy-start.2
  21.5 15.0 %copy-start.1 = (bf16[384,512]{1,0:T(8,128)(2,1)S(1)}, bf16[384,512]{1,0:T(8,128)(2,1)}, u32[]{:S(2)}) copy-start(bf16[384,512]{1,0:T(8,128)(2,1)} %constant.31.clone.table_any) | copy-start | bytes 1179652
  31.0 23.0 %all-to-all-start.1 = ((f32[16,1,8320]{2,1,0:T(1,128)}), f32[16,1,8320]{2,1,0:T(1,128)S(1)}, u32[]{:S(2)}, u32[]{:S(2)}) async-start(f32[16,1,8320]{2,1,0:T(1,128)} %bitcast.2), calls=%async_computation.1 | async-start | bytes 1064960 | tf_op jit(solution)/shard_map/all_to_all | solution.py:545
  36.6 1.1 %copy-start = (f32[1040,128]{1,0:T(8,128)S(1)}, f32[1040,128]{1,0:T(8,128)}, u32[]{:S(2)}) copy-start(f32[1040,128]{1,0:T(8,128)} %fields.1.after_any) | copy-start | bytes 1597444

commit v7 on v6

--- a/solution.py
+++ b/solution.py
@@ -260,7 +260,7 @@
             )
         )
     ]
-    for load in loads:
+    for load in loads[:6]:
         load.start()
     lane = lax.broadcasted_iota(jnp.int32, (BAND, WIDTH), 1)
     first_half = lane < BAND
@@ -270,6 +270,8 @@
     rows = 2 * ROWS
     for load in loads[:6]:
         load.wait()
+    for load in loads[6:]:
+        load.start()
     pupil_re, pupil_im = [jnp.concatenate([pupil_ref[n], pupil_ref[n]], 1) for n in range(2)]
     pupil_re_odd = jnp.where(first_half, -pupil_re, pupil_re)
     pupil_im_odd = jnp.where(first_half, -pupil_im, pupil_im)

time: 76.2 us -> 76.3 us (level)
  no operation moved by 1% of the time
where the time goes in v7:
time: 76.3 us; the launch traced here: 75.9 us
  blocking collectives  20.5 us (27%)
  waiting for transfers between devices  19.7 us (26%)
  Pallas kernels  17 us (22%)
  starting transfers between devices  15.8 us (21%)
  local copies, waits for them, and re-layouts  1.66 us (2%)
    all_to_all x1, blocking collectives, per_device(): term = lax.all_to_all(term, 'clip', 0, 0)  20.5 us
    all_to_all x1, waiting for transfers between devices, per_device(): chunks = lax.all_to_all(blocks.reshape(SRC, 1, CHUNK * WIDTH), 'src', 0, 0)  16.1 us
    all_to_all x1, starting transfers between devices, per_device(): points = lax.all_to_all(mine, 'src', 0, 0)  10.2 us
    pallas_call x1, Pallas kernels, per_device(): pl.pallas_call(main_kernel, in_specs=[free] * 4 + [hbm] * (len(stored) -...  9.44 us
    all_to_all x1, starting transfers between devices, per_device(): chunks = lax.all_to_all(blocks.reshape(SRC, 1, CHUNK * WIDTH), 'src', 0, 0)  5.55 us
    pallas_call x1, Pallas kernels, per_device(): pl.pallas_call(spectrum_kernel, in_specs=[hbm] * 3 + [free], out_specs=[f...  5.27 us
    all_to_all x1, waiting for transfers between devices, per_device(): points = lax.all_to_all(mine, 'src', 0, 0)  3.53 us
    unnamed x6, local copies, waits for them, and re-layouts  1.66 us
  transfers between devices with their start and end apart: 2, of which 2 were waited for; matrix products, arithmetic and copies ran while one was open for 0% of the time, Pallas kernels for 7%

profile of v7, /device:TPU:1, one launch (start us, length us, event | category | flops | bytes accessed | tf_op | source)
XLA Modules:
  0.0 75.9 jit_solution(2238000883292503034)
XLA Ops:
  0.6 1.3 %pack.1.after_any = f32[16,1,128]{2,1,0:T(1,128)} custom-call(s32[2]{0:T(128)} %index_ref.1, f32[2]{0:T(128)} %weight_ref.1), custom_call_target="tpu_custom_call" | custom-call | tf_op jit(solution)/shard_map/pack/pallas_call | solution.py:490
  1.9 10.2 %all-to-all-start = ((f32[16,1,128]{2,1,0:T(1,128)}), f32[16,1,128]{2,1,0:T(1,128)S(1)}, u32[]{:S(2)}, u32[]{:S(2)}) async-start(f32[16,1,128]{2,1,0:T(1,128)} %pack.1.after_any), calls=%async_computation | async-start | bytes 16384 | tf_op jit(solution)/shard_map/all_to_all | solution.py:496
  12.1 5.3 %spectrum.1 = (f32[2,128,128]{2,1,0:T(8,128)}, f32[2,128,128]{2,1,0:T(8,128)}) custom-call(f32[2,512,512]{2,1,0:T(8,128)} %mask_hbm.1, bf16[2,512,256]{2,1,0:T(8,128)(2,1)} %constant.22.clone.right_hbm.lines_hbm, bf16[2,256,512]{2,1,0:T(8,128)(2,1)} %constant.23.clone.left_hbm, f32[16,1,128]{2,1,0:T(1,128)} %pack.1.after_any), custom_call_target="tpu_custom_call" | custom-call | flops 2400000000 | bytes 3000000 | tf_op jit(solution)/shard_map/spectrum/pallas_call | solution.py:500
  17.4 3.5 %all-to-all-done.point_hbm = f32[16,1,128]{2,1,0:T(1,128)S(1)} async-done(((f32[16,1,128]{2,1,0:T(1,128)}), f32[16,1,128]{2,1,0:T(1,128)S(1)}, u32[]{:S(2)}, u32[]{:S(2)}) %all-to-all-start) | async-done | bytes 8224 | tf_op jit(solution)/shard_map/all_to_all | solution.py:496
  21.0 0.0 copy-start.2
  21.0 0.6 copy-done.2
  21.5 0.0 copy-start.1
  21.5 9.4 %fields.1.after_any = f32[1040,128]{1,0:T(8,128)} custom-call(f32[16,1,128]{2,1,0:T(1,128)} %copy-done.2, s32[16]{0:T(128)} %count_hbm.1, f32[2,128,128]{2,1,0:T(8,128)} %get-tuple-element.6.re_hbm, f32[2,128,128]{2,1,0:T(8,128)} %get-tuple-element.7.im_hbm, f32[2,64,64]{2,1,0:T(8,128)} %pupil_hbm.1, bf16[16,128,128]{2,1,0:T(8,128)(2,1)} %constant.24.clone.row_hbm, ...), custom_call_target="tpu_custom_call" | custom-call | flops 8000000000 | bytes 5000000 | tf_op jit(solution)/shard_map/fields/pallas_call | solution.py:523
  31.0 5.6 %all-to-all-start.1 = ((f32[16,1,8320]{2,1,0:T(1,128)}), f32[16,1,8320]{2,1,0:T(1,128)S(1)}, u32[]{:S(2)}, u32[]{:S(2)}) async-start(f32[16,1,8320]{2,1,0:T(1,128)} %bitcast.2), calls=%async_computation.1 | async-start | bytes 1064960 | tf_op jit(solution)/shard_map/all_to_all | solution.py:547
  36.6 0.0 copy-done.1
  36.6 0.0 copy-start
  36.6 1.1 %copy-done = f32[1040,128]{1,0:T(8,128)S(1)} copy-done((f32[1040,128]{1,0:T(8,128)S(1)}, f32[1040,128]{1,0:T(8,128)}, u32[]{:S(2)}) %copy-start) | copy-done | bytes 532504
  37.6 0.2 table.1.table_ref
  37.8 16.1 %all-to-all-done.1 = f32[16,1,8320]{2,1,0:T(1,128)S(1)} async-done(((f32[16,1,8320]{2,1,0:T(1,128)}), f32[16,1,8320]{2,1,0:T(1,128)S(1)}, u32[]{:S(2)}, u32[]{:S(2)}) %all-to-all-start.1) | async-done | bytes 532512 | tf_op jit(solution)/shard_map/all_to_all | solution.py:547
  54.0 0.9 %image.1 = (f32[2,32,512]{2,1,0:T(8,128)}, f32[32,1,128]{2,1,0:T(1,128)S(1)}) custom-call(f32[1040,128]{1,0:T(8,128)S(1)} %bitcast.3, bf16[384,512]{1,0:T(8,128)(2,1)S(1)} %table.1.table_ref), custom_call_target="tpu_custom_call" | custom-call | flops 100000000 | bytes 1000000 | tf_op jit(solution)/shard_map/image/pallas_call | solution.py:559
  54.8 20.5 %all_to_all.15 = f32[32,1,128]{2,1,0:T(1,128)S(1)} all-to-all(f32[32,1,128]{2,1,0:T(1,128)S(1)} %get-tuple-element.9), channel_id=1, replica_groups=mesh['clip'=32,'src'=16] {'clip'}, dimensions={0} | all-to-all | bytes 32768 | tf_op jit(solution)/shard_map/all_to_all | solution.py:571
  75.3 0.6 slice_reduce_fusion
Async XLA Ops:
  1.9 19.0 %all-to-all-start = ((f32[16,1,128]{2,1,0:T(1,128)}), f32[16,1,128]{2,1,0:T(1,128)S(1)}, u32[]{:S(2)}, u32[]{:S(2)}) async-start(f32[16,1,128]{2,1,0:T(1,128)} %pack.1.after_any), calls=%async_computation | async-start | bytes 16384 | tf_op jit(solution)/shard_map/all_to_all | solution.py:496
  21.0 0.6 copy-start.2
  21.5 15.0 %copy-start.1 = (bf16[384,512]{1,0:T(8,128)(2,1)S(1)}, bf16[384,512]{1,0:T(8,128)(2,1)}, u32[]{:S(2)}) copy-start(bf16[384,512]{1,0:T(8,128)(2,1)} %constant.31.clone.table_any) | copy-start | bytes 1179652
  31.0 23.0 %all-to-all-start.1 = ((f32[16,1,8320]{2,1,0:T(1,128)}), f32[16,1,8320]{2,1,0:T(1,128)S(1)}, u32[]{:S(2)}, u32[]{:S(2)}) async-start(f32[16,1,8320]{2,1,0:T(1,128)} %bitcast.2), calls=%async_computation.1 | async-start | bytes 1064960 | tf_op jit(solution)/shard_map/all_to_all | solution.py:547
  36.6 1.1 %copy-start = (f32[1040,128]{1,0:T(8,128)S(1)}, f32[1040,128]{1,0:T(8,128)}, u32[]{:S(2)}) copy-start(f32[1040,128]{1,0:T(8,128)} %fields.1.after_any) | copy-start | bytes 1597444
